TPU v7x, 128 devices: a whole 4x4x4 slice. The times are simulated.
128 devices in a mesh: row: 16 (over z_lo, y, core), col: 8 (over z_hi, x).
Axes of the slice: x: 4, y: 4, z: 4 (z_hi: 2, z_lo: 2; z = z_hi * 2 + z_lo), core: 2. Of those that a mesh axis runs over, the one named last changes fastest.
Arguments:
- image: bfloat16 [512, 1024, 256], P('row', 'col'), may hold values from -60 to 60
- bn_gain: float32 [256], replicated, may hold values from 0.5 to 2
- bn_shift: float32 [256], replicated, may hold values from -3 to 3
- expand_weight: bfloat16 [256, 1024], replicated, may hold values from -0.375 to 0.375
- expand_bias: float32 [1024], replicated, may hold values from -3 to 3
- depth_kernel: bfloat16 [3, 3, 1024], replicated, may hold values from -2 to 2
- depth_bias: float32 [1024], replicated, may hold values from -3 to 3
- project_weight: bfloat16 [1024, 256], replicated, may hold values from -0.1875 to 0.1875
- norm_gain: float32 [2, 256], replicated, may hold values from 0.5 to 2
- qkv_weight: bfloat16 [2, 256, 768], replicated, may hold values from -7 to 7
- out_weight: bfloat16 [2, 256, 256], replicated, may hold values from -0.375 to 0.375
Outputs:
- features_out: bfloat16 [512, 1024, 256], P('row', 'col')
All inputs are finite; a program needn't handle non-finite values.
Results may differ from a plain program's by a relative error of at most 0.011.
Values may be sent and summed in bfloat16 or wider, within the bound.
No kernel may reach another device: no remote copies, remote signals or barrier semaphores. Data moves between devices by JAX's collectives and lax.ppermute only.
A program may use at most 128 MiB of HBM per device.

v0:
```python
import math

import jax
import jax.numpy as jnp
from jax import lax
from jax.sharding import PartitionSpec as P

HEADS = 8
WINDOW = 8
GRID_SIDE = 16


def padded(cells, sides, width):
    for axis, dim in sides:
        count = lax.axis_size(axis)
        ends = count - 1
        head = lax.slice_in_dim(cells, 0, width, axis=dim)
        tail = lax.slice_in_dim(cells, cells.shape[dim] - width, cells.shape[dim], axis=dim)
        cells = jnp.concatenate(
            [
                lax.ppermute(tail, axis, [(i, (i + 1) % count) for i in range(ends)]),
                cells,
                lax.ppermute(head, axis, [((i + 1) % count, i) for i in range(ends)]),
            ],
            axis=dim,
        )
    return cells


def layer_norm(values, gain):
    mean = jnp.mean(values, axis=-1, keepdims=True)
    centred = values - mean
    spread = jnp.mean(centred * centred, axis=-1, keepdims=True)
    return centred * lax.rsqrt(spread + 1e-05) * gain


def expand_pixels(pixels, bn_gain, bn_shift, expand_weight, expand_bias):
    shape = pixels.shape
    normed = (pixels.astype(jnp.float32) * bn_gain + bn_shift).astype(jnp.bfloat16)
    hidden = (
        jnp.dot(normed.reshape(-1, shape[-1]), expand_weight, preferred_element_type=jnp.float32)
        + expand_bias
    )
    return jax.nn.gelu(hidden).astype(jnp.bfloat16).reshape(shape[:-1] + (expand_weight.shape[1],))


def depth_project(framed, residual, depth_kernel, depth_bias, project_weight):
    height = residual.shape[0]
    width = residual.shape[1]
    kernel = depth_kernel.astype(jnp.float32)
    total = jnp.zeros((height, width, framed.shape[2]), jnp.float32)
    for down in range(3):
        for across in range(3):
            total = (
                total
                + framed[down : down + height, across : across + width].astype(jnp.float32)
                * kernel[down, across]
            )
    middle = jax.nn.gelu(total + depth_bias).astype(jnp.bfloat16)
    moved = jnp.dot(
        middle.reshape(height * width, -1), project_weight, preferred_element_type=jnp.float32
    )
    return (residual.astype(jnp.float32) + moved.reshape(height, width, -1)).astype(jnp.bfloat16)


def attend(tokens, gain, qkv_weight, out_weight):
    groups, length, chans = tokens.shape
    values = tokens.astype(jnp.float32)
    normed = layer_norm(values, gain).astype(jnp.bfloat16)
    proj = jnp.dot(
        normed.reshape(groups * length, chans), qkv_weight, preferred_element_type=jnp.float32
    ).astype(jnp.bfloat16)
    proj = proj.reshape(groups, length, 3, HEADS, chans // HEADS)
    query = proj[:, :, 0]
    keys = proj[:, :, 1]
    vals = proj[:, :, 2]
    scores = jnp.einsum("gqhd,gkhd->ghqk", query, keys, preferred_element_type=jnp.float32) * (
        chans // HEADS
    ) ** (-0.5)
    top = jnp.max(scores, axis=-1, keepdims=True)
    weights = jnp.exp(scores - top)
    probs = (weights / jnp.sum(weights, axis=-1, keepdims=True)).astype(jnp.bfloat16)
    mixed = jnp.einsum("ghqk,gkhd->gqhd", probs, vals, preferred_element_type=jnp.float32).astype(
        jnp.bfloat16
    )
    moved = jnp.dot(
        mixed.reshape(groups * length, chans), out_weight, preferred_element_type=jnp.float32
    )
    return (values + moved.reshape(groups, length, chans)).astype(jnp.bfloat16)


def attend_batched(tokens, gain, qkv_weight, out_weight, wanted):
    groups = tokens.shape[0]
    per_step = math.gcd(groups, wanted)
    stacked = tokens.reshape((groups // per_step, per_step) + tokens.shape[1:])

    def one_batch(batch):
        return attend(batch, gain, qkv_weight, out_weight)

    return lax.map(one_batch, stacked).reshape(tokens.shape)


def per_device(
    image,
    bn_gain,
    bn_shift,
    expand_weight,
    expand_bias,
    depth_kernel,
    depth_bias,
    project_weight,
    norm_gain,
    qkv_weight,
    out_weight,
):
    rows_dev, cols_dev, chans = image.shape
    row_count = lax.axis_size("row")
    col_count = lax.axis_size("col")
    strips = rows_dev // WINDOW

    def expand_strip(index):
        piece = lax.dynamic_slice_in_dim(image, index * WINDOW, WINDOW, 0)
        return expand_pixels(piece, bn_gain, bn_shift, expand_weight, expand_bias)

    hidden = lax.map(expand_strip, jnp.arange(strips)).reshape(rows_dev, cols_dev, -1)
    framed_all = padded(hidden, (("row", 0), ("col", 1)), 1)

    def mix_strip(index):
        framed = lax.dynamic_slice_in_dim(framed_all, index * WINDOW, WINDOW + 2, 0)
        residual = lax.dynamic_slice_in_dim(image, index * WINDOW, WINDOW, 0)
        return depth_project(framed, residual, depth_kernel, depth_bias, project_weight)

    after_conv = lax.map(mix_strip, jnp.arange(strips)).reshape(rows_dev, cols_dev, chans)
    windows = after_conv.reshape(
        rows_dev // WINDOW, WINDOW, cols_dev // WINDOW, WINDOW, chans
    ).transpose(0, 2, 1, 3, 4)
    windows = windows.reshape(-1, WINDOW * WINDOW, chans)
    windows = attend_batched(windows, norm_gain[0], qkv_weight[0], out_weight[0], 16)
    after_block = windows.reshape(
        rows_dev // WINDOW, cols_dev // WINDOW, WINDOW, WINDOW, chans
    ).transpose(0, 2, 1, 3, 4)
    after_block = after_block.reshape(rows_dev, cols_dev, chans)
    rep_row = GRID_SIDE // row_count
    rep_col = GRID_SIDE // col_count
    low_row = rows_dev // GRID_SIDE
    low_col = cols_dev // GRID_SIDE
    items = low_row * low_col
    local = rep_row * rep_col
    devices = row_count * col_count
    arranged = after_block.reshape(
        rep_row, row_count, low_row, rep_col, col_count, low_col, chans
    ).transpose(1, 4, 2, 5, 0, 3, 6)
    outgoing = arranged.reshape(devices, 1, items, local, chans)
    received = lax.all_to_all(outgoing, ("row", "col"), split_axis=0, concat_axis=1, tiled=True)
    count = received.shape[2]
    tokens = (
        received.reshape(devices, count, local, chans)
        .transpose(1, 0, 2, 3)
        .reshape(count, devices * local, chans)
    )
    done = attend_batched(tokens, norm_gain[1], qkv_weight[1], out_weight[1], 2)
    reply = (
        done.reshape(count, devices, local, chans)
        .transpose(1, 0, 2, 3)
        .reshape(1, devices, count, local, chans)
    )
    returned = lax.all_to_all(reply, ("row", "col"), split_axis=1, concat_axis=0, tiled=True)
    placed = returned.reshape(
        row_count, col_count, low_row, low_col, rep_row, rep_col, chans
    ).transpose(4, 0, 2, 5, 1, 3, 6)
    return placed.reshape(rows_dev, cols_dev, chans)


def solution(mesh):
    in_specs = (P("row", "col", None), P(), P(), P(), P(), P(), P(), P(), P(), P(), P())
    out_specs = P("row", "col", None)
    return jax.shard_map(
        per_device, mesh=mesh, in_specs=in_specs, out_specs=out_specs, check_vma=False
    )
```

profile of v0, /device:TPU:1, one launch (start us, length us, event | category | flops | bytes accessed | tf_op | source)
XLA Modules:
  0.0 374.6 jit_solution(1689329970207599533)
XLA Ops:
  0.0 26.7 %while.40 = (s32[]{:T(128)}, bf16[4,8,128,1024]{3,2,1,0:T(8,128)(2,1)}, s32[4]{0:T(128)S(1)}, bf16[32,128,256]{2,1,0:T(8,128)(2,1)}, f32[256]{0:T(256)}, /*index...) while((s32[]{:T(128)}, ...), condition=%wide.region_1.2_spmd, body=%wide.region_0.1_spmd.sunk | while | flops 548405248 | bytes 8395443 | solution.py:125
  27.8 4.6 %collective-permute-start = (bf16[1,128,1024]{2,1,0:T(8,128)(2,1)S(1)}, bf16[1,128,1024]{2,1,0:T(8,128)(2,1)S(1)}, u32[]{:S(2)}, u32[]{:S(2)}) collective-permute-start(bf16[1,128,1024]{2,1,0:T(8,128)(2,1)S(1)} %get-tuple-element.248), channel_id=1, source_target_pairs={{0,8},{8,16},{16,24},{24,32},{32,40},{40,48},{48,56},{56,64},{64,7... | collective-permute-start | bytes 786440 | tf_op jit(solution)/shard_map/ppermute | solution.py:21
  35.9 4.2 %collective-permute-done.1 = bf16[1,128,1024]{2,1,0:T(8,128)(2,1)S(1)} collective-permute-done((bf16[1,128,1024]{2,1,0:T(8,128)(2,1)S(1)}, bf16[1,128,1024]{2,1,0:T(8,128)(2,1)S(1)}, u32[]{:S(2)}, u32[]{:S(2)}) %collective-permute-start.1) | collective-permute-done | bytes 262176 | tf_op jit(solution)/shard_map/ppermute | solution.py:23
  41.5 3.1 collective-permute-start.2
  46.6 3.8 %collective-permute-done.3 = bf16[34,1,1024]{2,1,0:T(2,128)(2,1)S(1)} collective-permute-done((bf16[34,1,1024]{2,1,0:T(2,128)(2,1)S(1)}, bf16[34,1,1024]{2,1,0:T(2,128)(2,1)S(1)}, u32[]{:S(2)}, u32[]{:S(2)}) %collective-permute-start.3) | collective-permute-done | bytes 69664 | tf_op jit(solution)/shard_map/ppermute | solution.py:23
  50.4 12.3 %pad_maximum_fusion = bf16[34,130,1024]{2,1,0:T(8,128)(2,1)} fusion(bf16[34,1,1024]{2,1,0:T(2,128)(2,1)S(1)} %collective-permute-done.3, bf16[1,128,1024]{2,1,0:T(8,128)(2,1)S(1)} %collective-permute-done.1, bf16[32,128,1024]{2,1,0:T(8,128)(2,1)} %bitcast.35, bf16[1,128,1024]{2,1,0:T(8,128)(2,1)S(1)} %collective-permute-done, ...), kind=kLoop, calls=%fused_computation.92 | loop fusion | flops 45260800 | bytes 18104320 | tf_op jit(solution)/shard_map/concatenate | solution.py:19
  62.7 63.0 %while.41 = (s32[]{:T(128)}, bf16[4,8,128,256]{3,2,1,0:T(8,128)(2,1)}, s32[4]{0:T(128)S(1)}, bf16[32,128,256]{2,1,0:T(8,128)(2,1)}, bf16[34,130,1024]{2,1,0:T(8,...) while((s32[]{:T(128)}, ...), condition=%wide.region_3.4_spmd, body=%wide.region_2.3_spmd.sunk | while | flops 575406080 | bytes 20562728 | solution.py:133
  63.9 15.2 %fusion.126 = bf16[4,8,128,256]{3,2,1,0:T(8,128)(2,1)} fusion(bf16[4,8,128,256]{3,2,1,0:T(8,128)(2,1)} %get-tuple-element.522, s32[]{:T(128)} %get-tuple-element.521, bf16[34,130,1024]{2,1,0:T(8,128)(2,1)} %get-tuple-element.540, s32[]{:T(128)S(6)} %add.362, s32[]{:T(128)S(6)} %add.363, s32[]{:T(128)S(6)} %add.364, s32[]{:T(128)S(6)} %add.365, ...), kind=kOutput, calls=%fused_computation.24.clone.1 | convolution fusion | flops 575406080 | bytes 20488728 | tf_op jit(solution)/shard_map/while/body/eval_jaxpr/dot_general | solution.py:60
  80.3 13.9 %fusion.126 = bf16[4,8,128,256]{3,2,1,0:T(8,128)(2,1)} fusion(bf16[4,8,128,256]{3,2,1,0:T(8,128)(2,1)} %get-tuple-element.522, s32[]{:T(128)} %get-tuple-element.521, bf16[34,130,1024]{2,1,0:T(8,128)(2,1)} %get-tuple-element.540, s32[]{:T(128)S(6)} %add.362, s32[]{:T(128)S(6)} %add.363, s32[]{:T(128)S(6)} %add.364, s32[]{:T(128)S(6)} %add.365, ...), kind=kOutput, calls=%fused_computation.24.clone.1 | convolution fusion | flops 575406080 | bytes 20488728 | tf_op jit(solution)/shard_map/while/body/eval_jaxpr/dot_general | solution.py:60
  95.4 14.7 %fusion.126 = bf16[4,8,128,256]{3,2,1,0:T(8,128)(2,1)} fusion(bf16[4,8,128,256]{3,2,1,0:T(8,128)(2,1)} %get-tuple-element.522, s32[]{:T(128)} %get-tuple-element.521, bf16[34,130,1024]{2,1,0:T(8,128)(2,1)} %get-tuple-element.540, s32[]{:T(128)S(6)} %add.362, s32[]{:T(128)S(6)} %add.363, s32[]{:T(128)S(6)} %add.364, s32[]{:T(128)S(6)} %add.365, ...), kind=kOutput, calls=%fused_computation.24.clone.1 | convolution fusion | flops 575406080 | bytes 20488728 | tf_op jit(solution)/shard_map/while/body/eval_jaxpr/dot_general | solution.py:60
  111.2 14.5 %fusion.126 = bf16[4,8,128,256]{3,2,1,0:T(8,128)(2,1)} fusion(bf16[4,8,128,256]{3,2,1,0:T(8,128)(2,1)} %get-tuple-element.522, s32[]{:T(128)} %get-tuple-element.521, bf16[34,130,1024]{2,1,0:T(8,128)(2,1)} %get-tuple-element.540, s32[]{:T(128)S(6)} %add.362, s32[]{:T(128)S(6)} %add.363, s32[]{:T(128)S(6)} %add.364, s32[]{:T(128)S(6)} %add.365, ...), kind=kOutput, calls=%fused_computation.24.clone.1 | convolution fusion | flops 575406080 | bytes 20488728 | tf_op jit(solution)/shard_map/while/body/eval_jaxpr/dot_general | solution.py:60
  127.6 73.0 %while.42 = (s32[]{:T(128)}, bf16[4,16,64,256]{3,2,1,0:T(8,128)(2,1)}, bf16[4,16,64,256]{3,2,1,0:T(8,128)(2,1)S(1)}, f32[1,256]{1,0:T(1,128)S(1)}, bf16[256,768]...) while((s32[]{:T(128)}, bf16[4,16,64,256]{3,2,1,0:T(8,128)(2,1)}, ...), condition=%wide.region_9.10_spmd, body=%wide.region_4.9_spmd.sunk | while | flops 611845184 | bytes 43636396 | solution.py:100
  131.2 4.1 %reshape.137 = bf16[16,64,3,8,32]{1,0,4,3,2:T(8,128)(2,1)S(1)} reshape(bf16[1024,768]{0,1:T(8,128)(2,1)} %copy.140) | data formatting | bytes 3145728 | tf_op jit(solution)/shard_map/while/body/eval_jaxpr/reshape | solution.py:73
  136.8 6.2 %fusion.135 = (f32[16,8,64]{2,1,0:T(8,128)S(1)}, f32[16,8,64,64]{2,3,1,0:T(8,128)S(1)}) fusion(f32[16,8,64,64]{2,3,1,0:T(8,128)S(1)} %fusion.134), kind=kOutput, calls=%fused_computation.104.clone.1 | output fusion | flops 2097215 | bytes 4227072 | tf_op jit(solution)/shard_map/while/body/eval_jaxpr/sub | solution.py:81
  149.4 4.1 %reshape.137 = bf16[16,64,3,8,32]{1,0,4,3,2:T(8,128)(2,1)S(1)} reshape(bf16[1024,768]{0,1:T(8,128)(2,1)} %copy.140) | data formatting | bytes 3145728 | tf_op jit(solution)/shard_map/while/body/eval_jaxpr/reshape | solution.py:73
  155.1 6.2 %fusion.135 = (f32[16,8,64]{2,1,0:T(8,128)S(1)}, f32[16,8,64,64]{2,3,1,0:T(8,128)S(1)}) fusion(f32[16,8,64,64]{2,3,1,0:T(8,128)S(1)} %fusion.134), kind=kOutput, calls=%fused_computation.104.clone.1 | output fusion | flops 2097215 | bytes 4227072 | tf_op jit(solution)/shard_map/while/body/eval_jaxpr/sub | solution.py:81
  167.7 4.1 %reshape.137 = bf16[16,64,3,8,32]{1,0,4,3,2:T(8,128)(2,1)S(1)} reshape(bf16[1024,768]{0,1:T(8,128)(2,1)} %copy.140) | data formatting | bytes 3145728 | tf_op jit(solution)/shard_map/while/body/eval_jaxpr/reshape | solution.py:73
  173.3 6.2 %fusion.135 = (f32[16,8,64]{2,1,0:T(8,128)S(1)}, f32[16,8,64,64]{2,3,1,0:T(8,128)S(1)}) fusion(f32[16,8,64,64]{2,3,1,0:T(8,128)S(1)} %fusion.134), kind=kOutput, calls=%fused_computation.104.clone.1 | output fusion | flops 2097215 | bytes 4227072 | tf_op jit(solution)/shard_map/while/body/eval_jaxpr/sub | solution.py:81
  185.9 4.1 %reshape.137 = bf16[16,64,3,8,32]{1,0,4,3,2:T(8,128)(2,1)S(1)} reshape(bf16[1024,768]{0,1:T(8,128)(2,1)} %copy.140) | data formatting | bytes 3145728 | tf_op jit(solution)/shard_map/while/body/eval_jaxpr/reshape | solution.py:73
  191.6 6.2 %fusion.135 = (f32[16,8,64]{2,1,0:T(8,128)S(1)}, f32[16,8,64,64]{2,3,1,0:T(8,128)S(1)}) fusion(f32[16,8,64,64]{2,3,1,0:T(8,128)S(1)} %fusion.134), kind=kOutput, calls=%fused_computation.104.clone.1 | output fusion | flops 2097215 | bytes 4227072 | tf_op jit(solution)/shard_map/while/body/eval_jaxpr/sub | solution.py:81
  204.1 13.9 %all-to-all-start = ((bf16[128,1,16,2,256]{4,2,3,1,0:T(8,128)(2,1)}), bf16[128,1,16,2,256]{4,2,3,1,0:T(8,128)(2,1)S(1)}, u32[]{:S(2)}, u32[]{:S(2)}) async-start(bf16[128,1,16,2,256]{4,2,3,1,0:T(8,128)(2,1)} %bitcast.265), calls=%async_computation | async-start | bytes 4194304 | tf_op jit(solution)/shard_map/all_to_all | solution.py:154
  218.1 29.0 %all-to-all-done = bf16[128,1,16,2,256]{4,2,3,1,0:T(8,128)(2,1)S(1)} async-done(((bf16[128,1,16,2,256]{4,2,3,1,0:T(8,128)(2,1)}), bf16[128,1,16,2,256]{4,2,3,1,0:T(8,128)(2,1)S(1)}, u32[]{:S(2)}, u32[]{:S(2)}) %all-to-all-start) | async-done | bytes 2097184 | tf_op jit(solution)/shard_map/all_to_all | solution.py:154
  249.3 84.1 %while.43 = (s32[]{:T(128)}, bf16[8,2,256,256]{3,2,1,0:T(8,128)(2,1)}, bf16[8,2,256,256]{3,1,0,2:T(2,128)(2,1)}, f32[1,256]{1,0:T(1,128)S(1)}, bf16[256,768]{1,0...) while((s32[]{:T(128)}, bf16[8,2,256,256]{3,2,1,0:T(8,128)(2,1)}, ...), condition=%wide.region_15.16_spmd, body=%wide.region_10.15_spmd.sunk | while | flops 410256128 | bytes 18150992 | solution.py:100
  252.7 3.5 fusion.146
  263.2 3.5 fusion.146
  273.7 3.5 fusion.146
  284.3 3.5 fusion.146
  294.8 3.5 fusion.146
  305.3 3.5 fusion.146
  315.8 3.5 fusion.146
  326.3 3.5 fusion.146
  338.4 34.6 %all_to_all.8 = bf16[1,128,16,2,256]{4,2,3,0,1:T(8,128)(2,1)S(1)} all-to-all(bf16[1,128,16,2,256]{4,2,3,0,1:T(8,128)(2,1)S(1)} %bitcast.267), channel_id=1, replica_groups=mesh['row'=16,'col'=8] {'row','col'}, dimensions={1} | all-to-all | bytes 4194304 | tf_op jit(solution)/shard_map/all_to_all | solution.py:167
  (250 shorter events, 135.9 us)
Async XLA Ops:
  0.0 34.3 %copy-start.6 = (bf16[2,256,256]{2,1,0:T(8,128)(2,1)S(1)}, bf16[2,256,256]{2,1,0:T(8,128)(2,1)}, u32[]{:S(2)}) copy-start(bf16[2,256,256]{2,1,0:T(8,128)(2,1)} %param.29) | copy-start | bytes 786436
  0.0 35.0 %copy-start.5 = (bf16[2,256,768]{2,1,0:T(8,128)(2,1)S(1)}, bf16[2,256,768]{2,1,0:T(8,128)(2,1)}, u32[]{:S(2)}) copy-start(bf16[2,256,768]{2,1,0:T(8,128)(2,1)} %param.28) | copy-start | bytes 2359300
  27.8 8.1 %collective-permute-start = (bf16[1,128,1024]{2,1,0:T(8,128)(2,1)S(1)}, bf16[1,128,1024]{2,1,0:T(8,128)(2,1)S(1)}, u32[]{:S(2)}, u32[]{:S(2)}) collective-permute-start(bf16[1,128,1024]{2,1,0:T(8,128)(2,1)S(1)} %get-tuple-element.248), channel_id=1, source_target_pairs={{0,8},{8,16},{16,24},{24,32},{32,40},{40,48},{48,56},{56,64},{64,7... | collective-permute-start | bytes 786440 | tf_op jit(solution)/shard_map/ppermute | solution.py:21
  32.4 7.7 %collective-permute-start.1 = (bf16[1,128,1024]{2,1,0:T(8,128)(2,1)S(1)}, bf16[1,128,1024]{2,1,0:T(8,128)(2,1)S(1)}, u32[]{:S(2)}, u32[]{:S(2)}) collective-permute-start(bf16[1,128,1024]{2,1,0:T(8,128)(2,1)S(1)} %get-tuple-element.249), channel_id=1, source_target_pairs={{8,0},{16,8},{24,16},{32,24},{40,32},{48,40},{56,48},{64,56},{72,6... | collective-permute-start | bytes 786440 | tf_op jit(solution)/shard_map/ppermute | solution.py:23
  35.9 10.3 %copy-start.8 = (f32[2,256]{1,0:T(2,128)S(1)}, f32[2,256]{1,0:T(2,128)}, u32[]{:S(2)}) copy-start(f32[2,256]{1,0:T(2,128)} %param.27) | copy-start | bytes 6148
  41.5 5.1 %collective-permute-start.2 = (bf16[34,1,1024]{2,1,0:T(2,128)(2,1)S(1)}, bf16[34,1,1024]{2,1,0:T(2,128)(2,1)S(1)}, u32[]{:S(2)}, u32[]{:S(2)}) collective-permute-start(bf16[34,1,1024]{2,1,0:T(2,128)(2,1)S(1)} %get-tuple-element.246), channel_id=1, source_target_pairs={{0,1},{1,2},{2,3},{3,4},{4,5},{5,6},{6,7},{8,9},{9,10},{10,11},{11... | collective-permute-start | bytes 208904 | tf_op jit(solution)/shard_map/ppermute | solution.py:21
  44.6 5.8 %collective-permute-start.3 = (bf16[34,1,1024]{2,1,0:T(2,128)(2,1)S(1)}, bf16[34,1,1024]{2,1,0:T(2,128)(2,1)S(1)}, u32[]{:S(2)}, u32[]{:S(2)}) collective-permute-start(bf16[34,1,1024]{2,1,0:T(2,128)(2,1)S(1)} %get-tuple-element.247), channel_id=1, source_target_pairs={{1,0},{2,1},{3,2},{4,3},{5,4},{6,5},{7,6},{9,8},{10,9},{11,10},{12... | collective-permute-start | bytes 208904 | tf_op jit(solution)/shard_map/ppermute | solution.py:23
  46.2 16.5 %copy-start.4 = (bf16[3,3,1024]{2,1,0:T(4,128)(2,1)S(1)}, bf16[3,3,1024]{2,1,0:T(4,128)(2,1)}, u32[]{:S(2)}) copy-start(bf16[3,3,1024]{2,1,0:T(4,128)(2,1)} %param.24) | copy-start | bytes 55300
  46.2 16.5 %copy-start.9 = (bf16[1024,256]{1,0:T(8,128)(2,1)S(1)}, bf16[1024,256]{1,0:T(8,128)(2,1)}, u32[]{:S(2)}) copy-start(bf16[1024,256]{1,0:T(8,128)(2,1)} %param.26) | copy-start | bytes 1572868
  46.2 16.5 %copy-start.10 = (f32[1024]{0:T(1024)S(1)}, f32[1024]{0:T(1024)}, u32[]{:S(2)}) copy-start(f32[1024]{0:T(1024)} %param.25) | copy-start | bytes 12292
  127.6 1.3 copy-start
  143.0 1.6 copy-start.1
  143.0 1.6 copy-start.3
  145.9 1.3 copy-start
  161.2 1.6 copy-start.1
  161.2 1.6 copy-start.3
  164.1 1.3 copy-start
  179.5 1.6 copy-start.1
  179.5 1.6 copy-start.3
  182.4 1.3 copy-start
  197.7 1.6 copy-start.1
  197.7 1.6 copy-start.3
  204.1 45.1 %copy-start.2 = (bf16[256,768]{1,0:T(8,128)(2,1)S(1)}, bf16[256,768]{1,0:T(8,128)(2,1)}, u32[]{:S(2)}) copy-start(bf16[256,768]{1,0:T(8,128)(2,1)} %get-tuple-element.576) | copy-start | bytes 1179652
  204.1 45.1 %copy-start.7 = (bf16[256,256]{1,0:T(8,128)(2,1)S(1)}, bf16[256,256]{1,0:T(8,128)(2,1)}, u32[]{:S(2)}) copy-start(bf16[256,256]{1,0:T(8,128)(2,1)} %get-tuple-element.577) | copy-start | bytes 393220
  204.1 42.9 %all-to-all-start = ((bf16[128,1,16,2,256]{4,2,3,1,0:T(8,128)(2,1)}), bf16[128,1,16,2,256]{4,2,3,1,0:T(8,128)(2,1)S(1)}, u32[]{:S(2)}, u32[]{:S(2)}) async-start(bf16[128,1,16,2,256]{4,2,3,1,0:T(8,128)(2,1)} %bitcast.265), calls=%async_computation | async-start | bytes 4194304 | tf_op jit(solution)/shard_map/all_to_all | solution.py:154
where the time goes:
time: 376 us; the launch traced here: 375 us
  matrix products  142 us (38%)
  local copies, waits for them, and re-layouts  77.4 us (21%)
  other arithmetic  51.8 us (14%)
  waiting for transfers between devices  37.4 us (10%)
  blocking collectives  34.6 us (9%)
  starting transfers between devices  25 us (7%)
  loops' own time  5.88 us (2%)
    dot_general x4, matrix products, depth_project(): jnp.dot(middle.reshape(height * width, -1), project_weight, preferred_ele...  58.2 us
    all_to_all x1, blocking collectives, per_device(): lax.all_to_all(reply, ('row', 'col'), split_axis=1, concat_axis=0, tiled=...  34.6 us
    all_to_all x1, waiting for transfers between devices, per_device(): lax.all_to_all(outgoing, ('row', 'col'), split_axis=0, concat_axis=1, til...  29 us
    sub x8, matrix products, attend(): weights = jnp.exp(scores - top)  27.8 us
    sub x4, other arithmetic, attend(): weights = jnp.exp(scores - top)  24.6 us
    dot_general x12, matrix products, attend(): jnp.einsum('ghqk,gkhd->gqhd', probs, vals, preferred_element_type=jnp.flo...  23.7 us
    reshape x12, local copies, waits for them, and re-layouts, attend(): proj = proj.reshape(groups, length, 3, HEADS, chans // HEADS)  17.9 us
    all_to_all x1, starting transfers between devices, per_device(): lax.all_to_all(outgoing, ('row', 'col'), split_axis=0, concat_axis=1, til...  13.9 us
  transfers between devices with their start and end apart: 5, of which 4 were waited for; matrix products, arithmetic and copies ran while one was open for 0% of the time, Pallas kernels for 0%

commit v1 on v0

v1 whole, which is shorter than its diff:
```python
import jax
import jax.numpy as jnp
from jax import lax
from jax.experimental import pallas as pl
from jax.experimental.pallas import tpu as pltpu
from jax.sharding import PartitionSpec as P

HEADS = 8
HEAD = 32
CH = 256
HID = 1024
WINDOW = 8
EPS = 1e-5
GELU_A = 0.7978845608028654
GELU_B = 0.7978845608028654 * 0.044715
QSCALE = 32.0**-0.5 * 1.4426950408889634
BF = jnp.bfloat16
F32 = jnp.float32


def mm(a, b, dims):
    return lax.dot_general(a, b, (dims, ((), ())), preferred_element_type=F32)


def nn(a, b):
    return mm(a, b, ((1,), (0,)))


def nt(a, b):
    return mm(a, b, ((1,), (1,)))


def tn(a, b):
    return mm(a, b, ((0,), (0,)))


def twice_gelu(x):
    inner = x * (x * x * jnp.asarray(GELU_B, x.dtype) + jnp.asarray(GELU_A, x.dtype))
    return x + x * jnp.tanh(inner)


def normalised(y, gain):
    mean = jnp.mean(y, axis=-1, keepdims=True)
    centred = y - mean
    spread = jnp.mean(centred * centred, axis=-1, keepdims=True)
    return centred * lax.rsqrt(spread + EPS) * gain


def store_halves(ref, at, values):
    ref[0, at, :] = values[:, :128]
    ref[1, at, :] = values[:, 128:]


def load_halves(ref, at):
    return jnp.concatenate([ref[0, at, :], ref[1, at, :]], axis=1)


def qkv_of(xn, wk, wqv):
    keys = nn(xn, wk).astype(BF)
    turned = nt(wqv, xn)
    return (turned[:CH] * QSCALE).astype(BF), keys, turned[CH:].astype(BF)


def window_mix(xn, wk, wqv):
    query, keys, vals = qkv_of(xn, wk, wqv)
    lane = lax.broadcasted_iota(jnp.int32, (HEAD, 128), 1)
    first = lane < 64
    first_keys = lax.broadcasted_iota(jnp.int32, (64, 128), 1) < 64
    none = jnp.zeros((HEAD, 128), BF)
    ones = jnp.ones((16, 128), BF)
    pairs = []
    for p in range(2):
        rows = []
        for g in range(2):
            lhs = jnp.concatenate(
                [
                    keys[128 * p : 128 * p + 64, 128 * g : 128 * g + 128],
                    keys[128 * p + 64 : 128 * p + 128, 128 * g : 128 * g + 128],
                ],
                axis=1,
            )
            cols = []
            for j in range(4):
                h = 4 * g + j
                q = query[HEAD * h : HEAD * h + HEAD, 128 * p : 128 * p + 128]
                parts = [none] * 8
                parts[j] = jnp.where(first, q, none)
                parts[4 + j] = jnp.where(first, none, q)
                cols.append(jnp.concatenate(parts, axis=0))
            scores = nn(lhs, jnp.concatenate(cols, axis=1))
            top = jnp.max(scores, axis=0, keepdims=True)
            probs = jnp.exp2((scores - top).astype(BF))
            for j in range(0, 4, 2):
                h = 4 * g + j
                blocks = []
                for i in range(2):
                    ph = probs[:, 128 * (j + i) : 128 * (j + i) + 128]
                    zero = jnp.zeros_like(ph)
                    blocks.append(
                        jnp.concatenate(
                            [jnp.where(first_keys, ph, zero), jnp.where(first_keys, zero, ph)], axis=0
                        )
                    )
                left = jnp.concatenate(
                    [vals[HEAD * h : HEAD * h + 2 * HEAD, 128 * p : 128 * p + 128], ones], axis=0
                )
                out = nn(left, jnp.concatenate(blocks, axis=1))
                inv = 1.0 / out[64:65]
                rows.append((out[:32, :128] * inv[:, :128]).astype(BF))
                rows.append((out[32:64, 128:] * inv[:, 128:]).astype(BF))
        pairs.append(jnp.concatenate(rows, axis=0))
    return jnp.concatenate(pairs, axis=1)


def grid_mix(xn, wk, wqv):
    query, keys, vals = qkv_of(xn, wk, wqv)
    none = jnp.zeros((HEAD, 256), BF)
    ones = jnp.ones((16, 256), BF)
    rows = []
    for h in range(HEADS):
        g, j = divmod(h, 4)
        parts = [none] * 4
        parts[j] = query[HEAD * h : HEAD * h + HEAD]
        scores = nn(keys[:, 128 * g : 128 * g + 128], jnp.concatenate(parts, axis=0))
        top = jnp.max(scores, axis=0, keepdims=True)
        probs = jnp.exp2((scores - top).astype(BF))
        out = nn(jnp.concatenate([vals[HEAD * h : HEAD * h + HEAD], ones], axis=0), probs)
        rows.append((out[:HEAD] * (1.0 / out[HEAD : HEAD + 1])).astype(BF))
    return jnp.concatenate(rows, axis=0)


def front_kernel(
    edge_ref,
    image_ref,
    above_ref,
    below_ref,
    sides_ref,
    bn_gain_ref,
    bn_shift_ref,
    expand_ref,
    expand_bias_ref,
    depth_ref,
    depth_bias_ref,
    project_ref,
    gain_ref,
    wk_ref,
    wqv_ref,
    wo_ref,
    out_ref,
    line,
    hidden,
    side_hidden,
    middle,
    moved,
):
    step = pl.program_id(0)
    strips = pl.num_programs(0)
    rows_dev = image_ref.shape[0]
    cell = lax.broadcasted_iota(jnp.int32, (16, 1), 0)

    def normed(values):
        return values.astype(F32) * bn_gain_ref[...] + bn_shift_ref[...]

    def activated(cells, c):
        lanes = slice(256 * c, 256 * c + 256)
        total = nn(cells, expand_ref[:, lanes]) + expand_bias_ref[:, lanes]
        return twice_gelu(total.astype(BF))

    def expand_row(values, row, keep):
        store_halves(line, slice(None), normed(values))
        cells = jnp.concatenate(
            [load_halves(line, pl.ds(m, 16, stride=WINDOW)) for m in range(WINDOW)], axis=0
        ).astype(BF)
        for c in range(HID // 256):
            lanes = slice(256 * c, 256 * c + 256)
            act = activated(cells, c)
            if keep is not None:
                act = act * keep
            act = act.reshape(WINDOW, 16, 256)
            hidden[row, 1 : WINDOW + 1, :, lanes] = act
            left = pltpu.roll(act[WINDOW - 1].astype(F32), 1, 0)
            right = pltpu.roll(act[0].astype(F32), 15, 0)
            left = jnp.where(cell == 0, side_hidden[pl.ds(row, 1), lanes], left)
            right = jnp.where(cell == 15, side_hidden[pl.ds(40 + row, 1), lanes], right)
            hidden[row, 0, :, lanes] = left.astype(BF)
            hidden[row, WINDOW + 1, :, lanes] = right.astype(BF)

    @pl.when(step == 0)
    def _():
        cells = normed(sides_ref[...]).astype(BF)
        index = lax.broadcasted_iota(jnp.int32, (80, 1), 0)
        right = index >= 40
        row = jnp.where(right, index - 40, index)
        keep = jnp.where(right, edge_ref[3], edge_ref[2])
        keep = jnp.where(row == 0, keep * edge_ref[0], keep)
        keep = jnp.where(row == rows_dev + 1, keep * edge_ref[1], keep)
        keep = keep.astype(F32)
        for c in range(HID // 256):
            lanes = slice(256 * c, 256 * c + 256)
            side_hidden[:, lanes] = activated(cells, c).astype(F32) * keep
        expand_row(above_ref[...], 0, edge_ref[0].astype(F32).astype(BF))
        expand_row(image_ref[0], 1, None)

    def expand_step(i, carry):
        expand_row(image_ref[step * WINDOW + 1 + i], step * WINDOW + 2 + i, None)
        return carry

    lax.fori_loop(0, jnp.where(step == strips - 1, WINDOW - 1, WINDOW), expand_step, 0)

    @pl.when(step == strips - 1)
    def _():
        expand_row(below_ref[...], rows_dev + 1, edge_ref[1].astype(F32).astype(BF))

    def depth_step(r, carry):
        for c in range(HID // 128):
            lanes = slice(128 * c, 128 * c + 128)
            total = None
            for down in range(3):
                around = hidden[step * WINDOW + r + down, :, :, lanes]
                for across in range(3):
                    term = around[across : across + WINDOW] * depth_ref[3 * down + across, :, lanes]
                    total = term if total is None else total + term
            act = twice_gelu(total + depth_bias_ref[:, lanes])
            middle[pl.ds(pl.multiple_of(r * 128, 128), 128), lanes] = act.reshape(128, 128)
        return carry

    lax.fori_loop(0, WINDOW, depth_step, 0)

    for part in range(4):
        at = slice(256 * part, 256 * part + 256)
        store_halves(moved, at, nn(middle[at, :], project_ref[...]))

    def quad_step(i, carry):
        pieces = []
        for p in range(2):
            col = pl.multiple_of(32 * i + 16 * p, 16)
            res = image_ref[pl.ds(step * WINDOW, WINDOW), pl.ds(col, 16), :].astype(F32)
            res = res.reshape(WINDOW, 2, WINDOW, CH)
            for w in range(2):
                conv = load_halves(moved, pl.ds(4 * i + 2 * p + w, 64, stride=16))
                pieces.append(res[:, w].reshape(64, CH) + conv)
        y = jnp.concatenate(pieces, axis=0)
        xn = normalised(y, gain_ref[...]).astype(BF)
        mixed = window_mix(xn, wk_ref[...], wqv_ref[...])
        y = (y + tn(mixed, wo_ref[...])).astype(BF)
        out_ref[0, pl.ds(4 * lax.rem(i, 2), 4), :, lax.div(i, 2)] = y.reshape(4, 4, 16, CH)
        return carry

    lax.fori_loop(0, 4, quad_step, 0)


def grid_kernel(tokens_ref, gain_ref, wk_ref, wqv_ref, wo_ref, out_ref, work):
    def norm_step(i, carry):
        at = pl.ds(pl.multiple_of(16 * i, 16), 16)
        y = tokens_ref[at].astype(F32).reshape(256, CH)
        rows = pl.ds(pl.multiple_of(256 * i, 256), 256)
        store_halves(work, rows, normalised(y, gain_ref[...]))
        return carry

    lax.fori_loop(0, 16, norm_step, 0)

    def set_step(k, carry):
        at = pl.ds(k, 256, stride=16)
        xn = load_halves(work, at).astype(BF)
        mixed = grid_mix(xn, wk_ref[...], wqv_ref[...])
        store_halves(work, at, tn(mixed, wo_ref[...]))
        return carry

    lax.fori_loop(0, 16, set_step, 0)

    def add_step(i, carry):
        at = pl.ds(pl.multiple_of(16 * i, 16), 16)
        y = load_halves(work, pl.ds(pl.multiple_of(256 * i, 256), 256)).reshape(16, 16, CH)
        out_ref[at] = (tokens_ref[at].astype(F32) + y).astype(BF)
        return carry

    lax.fori_loop(0, 16, add_step, 0)


def whole(shape):
    return pl.BlockSpec(shape, lambda i: (0,) * len(shape))


def front(edge, image, above, below, sides, params):
    rows_dev, cols_dev, chans = image.shape
    strips = rows_dev // WINDOW
    args = (image, above, below, sides) + params
    return pl.pallas_call(
        front_kernel,
        grid=(strips,),
        in_specs=[pl.BlockSpec(memory_space=pltpu.SMEM)] + [whole(a.shape) for a in args],
        out_specs=pl.BlockSpec((1, 8, 4, 2, 16, chans), lambda i: (i, 0, 0, 0, 0, 0)),
        out_shape=jax.ShapeDtypeStruct((strips, 8, 4, 2, 16, chans), BF),
        scratch_shapes=[
            pltpu.VMEM((2, cols_dev, 128), F32),
            pltpu.VMEM((rows_dev + 2, WINDOW + 2, 16, HID), BF),
            pltpu.VMEM((80, HID), F32),
            pltpu.VMEM((WINDOW * cols_dev, HID), BF),
            pltpu.VMEM((2, WINDOW * cols_dev, 128), F32),
        ],
        compiler_params=pltpu.CompilerParams(
            dimension_semantics=("arbitrary",), vmem_limit_bytes=48 * 2**20
        ),
        name="front",
    )(edge, *args)


def grid_attention(tokens, gain, wk, wqv, wo):
    args = (tokens, gain, wk, wqv, wo)
    return pl.pallas_call(
        grid_kernel,
        grid=(1,),
        in_specs=[whole(a.shape) for a in args],
        out_specs=whole(tokens.shape),
        out_shape=jax.ShapeDtypeStruct(tokens.shape, BF),
        scratch_shapes=[pltpu.VMEM((2, tokens.shape[0] * tokens.shape[1], 128), F32)],
        compiler_params=pltpu.CompilerParams(
            dimension_semantics=("arbitrary",), vmem_limit_bytes=40 * 2**20
        ),
        name="grid_attention",
    )(*args)


def halos(image):
    rows = lax.axis_size("row")
    cols = lax.axis_size("col")
    up = [(i, i + 1) for i in range(rows - 1)]
    down = [(i + 1, i) for i in range(rows - 1)]
    above = lax.ppermute(image[-1:], "row", up)
    below = lax.ppermute(image[:1], "row", down)
    first = jnp.concatenate([above[:, :1], image[:, :1], below[:, :1]], axis=0)[:, 0]
    last = jnp.concatenate([above[:, -1:], image[:, -1:], below[:, -1:]], axis=0)[:, 0]
    left = lax.ppermute(last, "col", [(i, i + 1) for i in range(cols - 1)])
    right = lax.ppermute(first, "col", [(i + 1, i) for i in range(cols - 1)])
    pad = ((0, 40 - left.shape[0]), (0, 0))
    sides = jnp.concatenate([jnp.pad(left, pad), jnp.pad(right, pad)], axis=0)
    return above[0], below[0], sides


def split_qkv(weight):
    wq, wk, wv = weight[:, :CH], weight[:, CH : 2 * CH], weight[:, 2 * CH :]
    return wk, jnp.concatenate([wq, wv], axis=1).T


def per_device(
    image,
    bn_gain,
    bn_shift,
    expand_weight,
    expand_bias,
    depth_kernel,
    depth_bias,
    project_weight,
    norm_gain,
    qkv_weight,
    out_weight,
):
    rows_dev, cols_dev, chans = image.shape
    row_at = lax.axis_index("row")
    col_at = lax.axis_index("col")
    edge = jnp.stack(
        [
            row_at > 0,
            row_at < lax.axis_size("row") - 1,
            col_at > 0,
            col_at < lax.axis_size("col") - 1,
        ]
    ).astype(jnp.int32)
    above, below, sides = halos(image)
    wk0, wqv0 = split_qkv(qkv_weight[0])
    wk1, wqv1 = split_qkv(qkv_weight[1])
    depth = jnp.broadcast_to((depth_kernel * 0.5).astype(BF).reshape(9, 1, HID), (9, 16, HID))
    params = (
        bn_gain[None],
        bn_shift[None],
        expand_weight,
        expand_bias[None],
        depth,
        jnp.broadcast_to(depth_bias.astype(BF)[None], (16, HID)),
        project_weight * jnp.asarray(0.5, BF),
        norm_gain[:1],
        wk0,
        wqv0,
        out_weight[0],
    )
    after_block = front(edge, image, above, below, sides, params)
    outgoing = after_block.reshape(128, 32, chans)
    received = lax.all_to_all(outgoing, ("row", "col"), split_axis=0, concat_axis=0, tiled=True)
    done = grid_attention(received.reshape(256, 16, chans), norm_gain[1:], wk1, wqv1, out_weight[1])
    returned = lax.all_to_all(
        done.reshape(128, 32, chans), ("row", "col"), split_axis=0, concat_axis=0, tiled=True
    )
    placed = returned.reshape(4, 8, 4, 2, 2, 8, chans).transpose(0, 2, 4, 3, 1, 5, 6)
    return placed.reshape(rows_dev, cols_dev, chans)


def solution(mesh):
    in_specs = (P("row", "col", None), P(), P(), P(), P(), P(), P(), P(), P(), P(), P())
    out_specs = P("row", "col", None)
    return jax.shard_map(
        per_device, mesh=mesh, in_specs=in_specs, out_specs=out_specs, check_vma=False
    )
```

time: 376 us -> 205 us (0.55)
  matrix products: 142 us -> 0 us
  Pallas kernels: 0 us -> 104 us
  local copies, waits for them, and re-layouts: 77.4 us -> 6.27 us
  other arithmetic: 51.8 us -> 2 us
  waiting for transfers between devices: 37.4 us -> 29.3 us
  loops' own time: 5.88 us -> 0 us
    dot_general x48 -> x0, matrix products: 114 us -> none  [the longest x4 58.2 us: depth_project(): jnp.dot(middle.reshape(height * width, -1), project_weight, preferred_ele...]
    pallas_call x0 -> x2, Pallas kernels: none -> 104 us  [the longest x1 56.7 us: front(): pl.pallas_call(front_kernel, grid=(strips,), in_specs=[pl.BlockSpec(memor...]
    sub x8 -> x0, matrix products: 27.8 us -> none  [attend(): weights = jnp.exp(scores - top)]
    sub x4 -> x0, other arithmetic: 24.6 us -> none  [attend(): weights = jnp.exp(scores - top)]
    reshape x12 -> x1, local copies, waits for them, and re-layouts: 17.9 us -> 1.6 us  [per_device(): returned.reshape(4, 8, 4, 2, 2, 8, chans).transpose(0, 2, 4, 3, 1, 5, 6)]
    dynamic_slice x16 -> x0, local copies, waits for them, and re-layouts: 13.9 us -> none  [the longest x8 9.05 us: attend_batched(): return lax.map(one_batch, stacked).reshape(tokens.shape)]
    concatenate x1, other arithmetic: 12.3 us -> 0.01 us  [halos(): sides = jnp.concatenate([jnp.pad(left, pad), jnp.pad(right, pad)], axis=0)]
    another operation x4 -> x0, local copies, waits for them, and re-layouts: 9.08 us -> none  [the longest x2 5 us: per_device(): done.reshape(count, devices, local, chans).transpose(1, 0, 2, 3)]
  transfers between devices with their start and end apart: 5 -> 5, of which waited for: 4 -> 2; matrix products, arithmetic and copies ran while one was open for 0% -> 3% of each run, Pallas kernels for 0% -> 0%
where the time goes in v1:
time: 205 us
  Pallas kernels  104 us (51%)
  blocking collectives  34.6 us (17%)
  waiting for transfers between devices  29.3 us (14%)
  starting transfers between devices  27.6 us (13%)
  local copies, waits for them, and re-layouts  6.27 us (3%)
    pallas_call x1, Pallas kernels, front(): pl.pallas_call(front_kernel, grid=(strips,), in_specs=[pl.BlockSpec(memor...  56.7 us
    pallas_call x1, Pallas kernels, grid_attention(): pl.pallas_call(grid_kernel, grid=(1,), in_specs=[whole(a.shape) for a in...  47.7 us
    all_to_all x1, blocking collectives, per_device(): lax.all_to_all(done.reshape(128, 32, chans), ('row', 'col'), split_axis=0...  34.6 us
    all_to_all x1, waiting for transfers between devices, per_device(): lax.all_to_all(outgoing, ('row', 'col'), split_axis=0, concat_axis=0, til...  28.6 us
    all_to_all x1, starting transfers between devices, per_device(): lax.all_to_all(outgoing, ('row', 'col'), split_axis=0, concat_axis=0, til...  15.9 us
    ppermute x1, starting transfers between devices, halos(): above = lax.ppermute(image[-1:], 'row', up)  4.59 us
  transfers between devices with their start and end apart: 5, of which 2 were waited for; matrix products, arithmetic and copies ran while one was open for 3% of the time, Pallas kernels for 0%

profile of v1, /device:TPU:1, one launch (start us, length us, event | category | flops | bytes accessed | tf_op | source)
XLA Modules:
  0.0 204.5 jit_solution(13840938703666820487)
XLA Ops:
  0.0 0.9 fusion.4
  0.9 0.1 copy.32
  1.0 4.6 %collective-permute-start = (bf16[1,128,256]{2,0,1:T(2,128)(2,1)S(1)}, bf16[1,128,256]{2,0,1:T(2,128)(2,1)S(1)}, u32[]{:S(2)}, u32[]{:S(2)}) collective-permute-start(bf16[1,128,256]{2,0,1:T(2,128)(2,1)S(1)} %copy.32), channel_id=1, source_target_pairs={{0,8},{8,16},{16,24},{24,32},{32,40},{40,48},{48,56},{56,64},{64,7... | collective-permute-start | bytes 196616 | tf_op jit(solution)/shard_map/ppermute | solution.py:329
  5.6 0.1 copy.33
  5.7 1.9 collective-permute-start.1
  7.6 1.0 fusion.3
  8.7 0.0 copy-start.4
  8.7 0.8 fusion.10
  9.5 0.8 broadcast_multiply_fusion.1
  10.3 1.0 slice_bitcast_fusion
  11.2 1.1 broadcast_multiply_fusion.project_ref
  12.3 0.0 copy-start.5
  12.4 0.0 copy-start
  12.4 0.0 copy-start.1
  12.4 0.0 copy-start.2
  12.4 0.0 copy-start.3
  12.4 0.1 fusion.5
  12.5 0.2 copy.36
  12.8 1.3 collective-permute-start.3
  14.1 4.0 %collective-permute-start.2 = (bf16[34,256]{1,0:T(8,128)(2,1)S(1)}, bf16[34,256]{1,0:T(8,128)(2,1)S(1)}, u32[]{:S(2)}, u32[]{:S(2)}) collective-permute-start(bf16[34,256]{1,0:T(8,128)(2,1)S(1)} %maximum_bitcast_fusion.2), channel_id=1, source_target_pairs={{0,1},{1,2},{2,3},{3,4},{4,5},{5,6},{6,7},{8,9},{9,10},{10,11},{11... | collective-permute-start | bytes 52232 | tf_op jit(solution)/shard_map/ppermute | solution.py:333
  18.1 0.1 add_convert_fusion.edge_ref
  18.2 0.1 copy.26.wk_ref
  18.4 0.0 collective-permute-done.3
  18.4 0.6 collective-permute-done.2
  19.1 56.7 %front.1 = bf16[4,8,4,2,16,256]{5,4,3,2,1,0:T(8,128)(2,1)} custom-call(s32[4]{0:T(128)S(1)} %add_convert_fusion.edge_ref, bf16[32,128,256]{2,1,0:T(8,128)(2,1)} %image_ref.1, bf16[128,256]{1,0:T(8,128)(2,1)S(1)} %bitcast.36, bf16[128,256]{1,0:T(8,128)(2,1)S(1)} %bitcast.37, bf16[80,256]{1,0:T(8,128)(2,1)S(1)} %fusion.2.sides_ref, f32[1,256]{1,0:T(1,128)S(1)} %bitcast.39, ...), custom_call_target="tpu_custom_call" | custom-call | tf_op jit(solution)/shard_map/front/pallas_call | solution.py:288
  75.8 15.9 %all-to-all-start = ((bf16[128,32,256]{2,1,0:T(8,128)(2,1)}), bf16[128,32,256]{2,1,0:T(8,128)(2,1)S(1)}, u32[]{:S(2)}, u32[]{:S(2)}) async-start(bf16[128,32,256]{2,1,0:T(8,128)(2,1)} %bitcast.12), calls=%async_computation | async-start | bytes 4194304 | tf_op jit(solution)/shard_map/all_to_all | solution.py:388
  91.6 0.2 copy.37
  91.8 0.1 copy.28.wk_ref
  92.0 28.6 %all-to-all-done = bf16[128,32,256]{2,1,0:T(8,128)(2,1)S(1)} async-done(((bf16[128,32,256]{2,1,0:T(8,128)(2,1)}), bf16[128,32,256]{2,1,0:T(8,128)(2,1)S(1)}, u32[]{:S(2)}, u32[]{:S(2)}) %all-to-all-start) | async-done | bytes 2097184 | tf_op jit(solution)/shard_map/all_to_all | solution.py:388
  120.6 47.7 %grid_attention.1 = bf16[256,16,256]{2,1,0:T(8,128)(2,1)S(1)} custom-call(bf16[256,16,256]{2,1,0:T(8,128)(2,1)S(1)} %bitcast.34, f32[1,256]{1,0:T(1,128)S(1)} %get-tuple-element.23.gain_ref, bf16[256,256]{1,0:T(8,128)(2,1)S(1)} %copy.28.wk_ref, bf16[512,256]{1,0:T(8,128)(2,1)S(1)} %maximum_bitcast_fusion.1.wqv_ref, bf16[256,256]{1,0:T(8,128)(2,1)S(1)} %get-tuple-element.17.wo_ref), custom_call_target="tpu_custom_call" | custom-call | tf_op jit(solution)/shard_map/grid_attention/pallas_call | solution.py:310
  168.3 34.6 %all_to_all.10 = bf16[128,32,256]{2,1,0:T(8,128)(2,1)S(1)} all-to-all(bf16[128,32,256]{2,1,0:T(8,128)(2,1)S(1)} %bitcast.35), channel_id=1, replica_groups=mesh['row'=16,'col'=8] {'row','col'}, dimensions={0} | all-to-all | bytes 4194304 | tf_op jit(solution)/shard_map/all_to_all | solution.py:390
  202.9 1.6 copy.29
  (25 shorter events, 0.2 us)
Async XLA Ops:
  1.0 11.7 %collective-permute-start = (bf16[1,128,256]{2,0,1:T(2,128)(2,1)S(1)}, bf16[1,128,256]{2,0,1:T(2,128)(2,1)S(1)}, u32[]{:S(2)}, u32[]{:S(2)}) collective-permute-start(bf16[1,128,256]{2,0,1:T(2,128)(2,1)S(1)} %copy.32), channel_id=1, source_target_pairs={{0,8},{8,16},{16,24},{24,32},{32,40},{40,48},{48,56},{56,64},{64,7... | collective-permute-start | bytes 196616 | tf_op jit(solution)/shard_map/ppermute | solution.py:329
  5.7 7.0 %collective-permute-start.1 = (bf16[1,128,256]{2,0,1:T(2,128)(2,1)S(1)}, bf16[1,128,256]{2,0,1:T(2,128)(2,1)S(1)}, u32[]{:S(2)}, u32[]{:S(2)}) collective-permute-start(bf16[1,128,256]{2,0,1:T(2,128)(2,1)S(1)} %copy.33), channel_id=1, source_target_pairs={{8,0},{16,8},{24,16},{32,24},{40,32},{48,40},{56,48},{64,56},{72,6... | collective-permute-start | bytes 196616 | tf_op jit(solution)/shard_map/ppermute | solution.py:330
  8.7 3.7 %copy-start.4 = (bf16[2,256,768]{2,1,0:T(8,128)(2,1)S(1)}, bf16[2,256,768]{2,1,0:T(8,128)(2,1)}, u32[]{:S(2)}) copy-start(bf16[2,256,768]{2,1,0:T(8,128)(2,1)} %param.20) | copy-start | bytes 2359300
  12.3 5.8 %copy-start.5 = (f32[1024]{0:T(1024)S(1)}, f32[1024]{0:T(1024)}, u32[]{:S(2)}) copy-start(f32[1024]{0:T(1024)} %param.17) | copy-start | bytes 12292
  12.4 6.7 %copy-start = (bf16[256,1024]{1,0:T(8,128)(2,1)S(1)}, bf16[256,1024]{1,0:T(8,128)(2,1)}, u32[]{:S(2)}) copy-start(bf16[256,1024]{1,0:T(8,128)(2,1)} %expand_ref.1) | copy-start | bytes 1572868
  12.4 6.7 %copy-start.1 = (f32[1024]{0:T(1024)S(1)}, f32[1024]{0:T(1024)}, u32[]{:S(2)}) copy-start(f32[1024]{0:T(1024)} %param.15) | copy-start | bytes 12292
  12.4 6.7 %copy-start.2 = (f32[256]{0:T(256)S(1)}, f32[256]{0:T(256)}, u32[]{:S(2)}) copy-start(f32[256]{0:T(256)} %param.12) | copy-start | bytes 3076
  12.4 6.7 %copy-start.3 = (f32[256]{0:T(256)S(1)}, f32[256]{0:T(256)}, u32[]{:S(2)}) copy-start(f32[256]{0:T(256)} %param.13) | copy-start | bytes 3076
  12.8 5.6 %collective-permute-start.3 = (bf16[34,256]{1,0:T(8,128)(2,1)S(1)}, bf16[34,256]{1,0:T(8,128)(2,1)S(1)}, u32[]{:S(2)}, u32[]{:S(2)}) collective-permute-start(bf16[34,256]{1,0:T(8,128)(2,1)S(1)} %maximum_bitcast_fusion.3), channel_id=1, source_target_pairs={{1,0},{2,1},{3,2},{4,3},{5,4},{6,5},{7,6},{9,8},{10,9},{11,10},{12... | collective-permute-start | bytes 52232 | tf_op jit(solution)/shard_map/ppermute | solution.py:334
  14.1 4.9 %collective-permute-start.2 = (bf16[34,256]{1,0:T(8,128)(2,1)S(1)}, bf16[34,256]{1,0:T(8,128)(2,1)S(1)}, u32[]{:S(2)}, u32[]{:S(2)}) collective-permute-start(bf16[34,256]{1,0:T(8,128)(2,1)S(1)} %maximum_bitcast_fusion.2), channel_id=1, source_target_pairs={{0,1},{1,2},{2,3},{3,4},{4,5},{5,6},{6,7},{8,9},{9,10},{10,11},{11... | collective-permute-start | bytes 52232 | tf_op jit(solution)/shard_map/ppermute | solution.py:333
  75.8 44.8 %all-to-all-start = ((bf16[128,32,256]{2,1,0:T(8,128)(2,1)}), bf16[128,32,256]{2,1,0:T(8,128)(2,1)S(1)}, u32[]{:S(2)}, u32[]{:S(2)}) async-start(bf16[128,32,256]{2,1,0:T(8,128)(2,1)} %bitcast.12), calls=%async_computation | async-start | bytes 4194304 | tf_op jit(solution)/shard_map/all_to_all | solution.py:388

commit v2 on v1

v2 whole, which is shorter than its diff:
```python
import jax
import jax.numpy as jnp
from jax import lax
from jax.experimental import pallas as pl
from jax.experimental.pallas import tpu as pltpu
from jax.sharding import PartitionSpec as P

HEADS = 8
SETS = 4
AHEAD = 4
WAHEAD = 2


HEAD = 32
CH = 256
HID = 1024
WINDOW = 8
EPS = 1e-5
GELU_A = 0.7978845608028654
CUBE = (GELU_A * 0.044715) ** (1.0 / 3.0)
GELU_C = GELU_A / CUBE
QSCALE = 32.0**-0.5 * 1.4426950408889634
BF = jnp.bfloat16
F32 = jnp.float32


def mm(a, b, dims):
    return lax.dot_general(a, b, (dims, ((), ())), preferred_element_type=F32)


def nn(a, b):
    return mm(a, b, ((1,), (0,)))


def nt(a, b):
    return mm(a, b, ((1,), (1,)))


def tn(a, b):
    return mm(a, b, ((0,), (0,)))


def scaled_gelu(z):
    return z + z * jnp.tanh(z * (z * z + GELU_C))


def normalised(y, gain):
    mean = jnp.mean(y, axis=-1, keepdims=True)
    centred = y - mean
    spread = jnp.mean(centred * centred, axis=-1, keepdims=True)
    return centred * lax.rsqrt(spread + EPS) * gain


def run(parts):
    while parts:
        left = []
        for part, n in parts:
            for _ in range(n):
                if next(part, part) is part:
                    break
            else:
                left.append((part, n))
        parts = left


def finish(part):
    run([(part, 1)])


def turned(weight):
    return weight.astype(F32).T.astype(BF)


def store_halves(ref, at, values):
    ref[0, at, :] = values[:, :128]
    ref[1, at, :] = values[:, 128:]


def load_halves(ref, at):
    return jnp.concatenate([ref[0, at, :], ref[1, at, :]], axis=1)


def window_mix(xn, wk, weight):
    pairs = xn.shape[0] // 128
    wqv = jnp.concatenate([weight[:, :CH], weight[:, 2 * CH :]], axis=1)
    proj = nn(xn, wqv)
    query = (proj[:, :CH] * QSCALE).astype(BF)
    vals = proj[:, CH:].astype(BF)
    yield
    keys = nt(wk, xn).astype(BF)
    yield
    none = jnp.zeros((HEAD, 128), BF)
    lane = lax.broadcasted_iota(jnp.int32, (128, 128), 1)
    row = lax.broadcasted_iota(jnp.int32, (128, 128), 0)
    inside = jnp.where(lane == jnp.where(row < 64, 0, 1), 1.0, 0.0).astype(BF)
    across = (row == 0) & (lane >= 64) | (row == 1) & (lane < 64)
    across = jnp.where(across, -1e30, 0.0).astype(BF)

    def score(t, g):
        cols = []
        for j in range(4):
            h = 4 * g + j
            parts = [none] * 4
            parts[j] = keys[HEAD * h : HEAD * h + HEAD, 128 * t : 128 * t + 128]
            parts.append(across)
            cols.append(jnp.concatenate(parts, axis=0))
        left = query[128 * t : 128 * t + 128, 128 * g : 128 * g + 128]
        left = jnp.concatenate([left, inside], axis=1)
        return nn(left, jnp.concatenate(cols, axis=1))

    order = [(t, g) for t in range(pairs) for g in range(2)]
    ahead = [score(*order[n]) for n in range(WAHEAD)]
    mixed = []
    for n, (t, g) in enumerate(order):
        scores = ahead.pop(0)
        if n + WAHEAD < len(order):
            ahead.append(score(*order[n + WAHEAD]))
        v = vals[128 * t : 128 * t + 128, 128 * g : 128 * g + 128]
        probs = []
        right = []
        for j in range(4):
            part = scores[:, 128 * j : 128 * j + 128]
            top = jnp.max(part, axis=1, keepdims=True)
            probs.append(jnp.exp2(part - top).astype(BF))
            mask = (lane >= HEAD * j) & (lane < HEAD * j + HEAD)
            zero = jnp.zeros_like(v)
            right.append(
                jnp.concatenate(
                    [jnp.where(mask, v, zero), jnp.where(mask, jnp.ones_like(v), zero)], axis=1
                )
            )
        out = nn(jnp.concatenate(probs, axis=1), jnp.concatenate(right, axis=0))
        mixed.append((out[:, :128] / out[:, 128:]).astype(BF))
        yield
    return jnp.concatenate(
        [jnp.concatenate(mixed[2 * t : 2 * t + 2], axis=1) for t in range(pairs)], axis=0
    )


def grid_mix(xns, wk, weight):
    zq = jnp.zeros((HEAD, 256), BF)
    lane = lax.broadcasted_iota(jnp.int32, (256, 128), 1)
    wqv = jnp.concatenate([weight[:, :CH], weight[:, 2 * CH :]], axis=1)
    proj = [nn(xn, wqv) for xn in xns]
    keysT = [nt(wk, xn).astype(BF) for xn in xns]
    query = [(p[:, :CH] * QSCALE).astype(BF) for p in proj]
    vals = [p[:, CH:].astype(BF) for p in proj]

    def score(t, h):
        g, j = divmod(h, 4)
        parts = [zq] * 4
        parts[j] = keysT[t][HEAD * h : HEAD * h + HEAD]
        return nn(query[t][:, 128 * g : 128 * g + 128], jnp.concatenate(parts, axis=0))

    order = [(t, h) for h in range(HEADS) for t in range(len(xns))]
    ahead = [score(*order[n]) for n in range(AHEAD)]
    halves = [[] for _ in xns]
    acc = [None for _ in xns]
    for n, (t, h) in enumerate(order):
        g, j = divmod(h, 4)
        scores = ahead.pop(0)
        if n + AHEAD < len(order):
            ahead.append(score(*order[n + AHEAD]))
        top = jnp.max(scores, axis=1, keepdims=True)
        probs = jnp.exp2(scores - top).astype(BF)
        mask = (lane >= HEAD * j) & (lane < HEAD * j + HEAD)
        v = vals[t][:, 128 * g : 128 * g + 128]
        z = jnp.zeros_like(v)
        right = jnp.concatenate([jnp.where(mask, v, z), jnp.where(mask, jnp.ones_like(v), z)], axis=1)
        out = nn(probs, right)
        acc[t] = out if j == 0 else acc[t] + out
        if j == 3:
            halves[t].append((acc[t][:, :128] / acc[t][:, 128:]).astype(BF))
    return [jnp.concatenate(x, axis=1) for x in halves]


def front_kernel(
    edge_ref,
    image_ref,
    above_ref,
    below_ref,
    sides_ref,
    bn_gain_ref,
    bn_shift_ref,
    expand_ref,
    expand_bias_ref,
    depth_ref,
    depth_bias_ref,
    project_ref,
    gain_ref,
    qkv_ref,
    wo_ref,
    out_ref,
    line,
    hidden,
    side_hidden,
    middle,
    moved,
    wk,
    taps,
):
    step = pl.program_id(0)
    rows_dev = image_ref.shape[0]
    strips = rows_dev // WINDOW
    cell = lax.broadcasted_iota(jnp.int32, (16, 1), 0)

    def normed(values):
        return values.astype(F32) * (bn_gain_ref[...] * CUBE) + bn_shift_ref[...] * CUBE

    def activated(cells, c):
        lanes = slice(256 * c, 256 * c + 256)
        total = nn(cells, expand_ref[:, lanes]) + expand_bias_ref[:, lanes] * CUBE
        return scaled_gelu(total)

    def put(row, at, c, values):
        hidden[2 * c, row, at] = values[..., :128].astype(hidden.dtype)
        hidden[2 * c + 1, row, at] = values[..., 128:].astype(hidden.dtype)

    def expand_rows(rows, first_row, keep_at, keep):
        count = len(rows)
        for n in range(count):
            store_halves(line, slice(128 * n, 128 * n + 128), normed(rows[n]))
        cells = jnp.concatenate(
            [
                load_halves(line, pl.ds(128 * n + m, 16, stride=WINDOW))
                for n in range(count)
                for m in range(WINDOW)
            ],
            axis=0,
        ).astype(BF)
        for c in range(HID // 256):
            lanes = slice(256 * c, 256 * c + 256)
            act = activated(cells, c).reshape(count, WINDOW, 16, 256)
            yield
            for n in range(count):
                one = act[n] * keep if n == keep_at else act[n]
                row = first_row + n
                put(row, slice(1, WINDOW + 1), c, one)
                left = pltpu.roll(one[WINDOW - 1], 1, 0)
                right = pltpu.roll(one[0], 15, 0)
                left = jnp.where(cell == 0, side_hidden[pl.ds(row, 1), lanes], left)
                right = jnp.where(cell == 15, side_hidden[pl.ds(40 + row, 1), lanes], right)
                put(row, 0, c, left)
                put(row, WINDOW + 1, c, right)

    @pl.when(step == 0)
    def _():
        wk[...] = turned(qkv_ref[0, :, CH : 2 * CH])
        for tap in range(9):
            row = depth_ref[tap // 3, tap % 3 : tap % 3 + 1].astype(F32) * 0.5
            taps[8 * tap : 8 * tap + 8, :] = jnp.broadcast_to(row, (8, HID))
        taps[72:80, :] = jnp.broadcast_to(depth_bias_ref[...] * CUBE, (8, HID))
        cells = normed(sides_ref[...]).astype(BF)
        index = lax.broadcasted_iota(jnp.int32, (80, 1), 0)
        right = index >= 40
        row = jnp.where(right, index - 40, index)
        keep = jnp.where(right, edge_ref[3], edge_ref[2])
        keep = jnp.where(row == 0, keep * edge_ref[0], keep)
        keep = jnp.where(row == rows_dev + 1, keep * edge_ref[1], keep)
        keep = keep.astype(F32)
        for c in range(HID // 256):
            lanes = slice(256 * c, 256 * c + 256)
            side_hidden[:, lanes] = activated(cells, c) * keep
        finish(expand_rows([above_ref[...], image_ref[0]], 0, 0, edge_ref[0].astype(F32)))

    def expand(strip, i):
        base = strip * WINDOW + 1 + 4 * i
        rows = [image_ref[base + n] for n in range(3)]
        last = base + 3
        beyond = last == rows_dev
        final = image_ref[jnp.minimum(last, rows_dev - 1)]
        rows.append(jnp.where(beyond, below_ref[...], final))
        keep = jnp.where(beyond, edge_ref[1], 1).astype(F32)
        yield from expand_rows(rows, base + 1, 3, keep)

    def depth(strip, r):
        at = pl.ds(pl.multiple_of(r * 128, 128), 128)
        for c in range(HID // 128):
            lanes = slice(128 * c, 128 * c + 128)
            total = None
            for down in range(3):
                around = hidden[c, strip * WINDOW + r + down]
                around = around.reshape(WINDOW + 2, 2, 8, 128)
                for across in range(3):
                    tap = 8 * (3 * down + across)
                    term = around[across : across + WINDOW] * taps[tap : tap + 8, lanes]
                    total = term if total is None else total + term
            act = scaled_gelu(total + taps[72:80, lanes])
            middle[at, lanes] = act.reshape(128, 128).astype(BF)
            yield

    def project(i):
        for n in range(4):
            at = pl.ds(pl.multiple_of(512 * i + 128 * n, 128), 128)
            store_halves(moved, at, nn(middle[at, :], project_ref[...]) * (0.5 / CUBE))
            yield

    def windows(strip, i):
        pieces = []
        for p in range(4):
            col = pl.multiple_of(64 * i + 16 * p, 16)
            res = image_ref[pl.ds(strip * WINDOW, WINDOW), pl.ds(col, 16), :].astype(F32)
            res = res.reshape(WINDOW, 2, WINDOW, CH)
            for w in range(2):
                conv = load_halves(moved, pl.ds(2 * (4 * i + p) + w, 64, stride=16))
                pieces.append(res[:, w].reshape(64, CH) + conv)
        y = jnp.concatenate(pieces, axis=0)
        xn = normalised(y, gain_ref[0:1]).astype(BF)
        yield
        mixed = yield from window_mix(xn, wk[...], qkv_ref[0])
        y = (y + nn(mixed, wo_ref[0])).astype(BF)
        out_ref[0, :, :, i] = y.reshape(8, 4, 16, CH)

    def halves(*parts):
        def body(i, carry):
            run([(part(i), n) for part, n in parts])
            return carry

        lax.fori_loop(0, 2, body, 0)

    def depth_half(i):
        for n in range(4):
            yield from depth(step, 4 * i + n)

    def windows_half(i):
        return windows(step - 1, i)

    def expand_half(i):
        return expand(step + 1, i)

    @pl.when(step == 0)
    def _():
        halves((lambda i: expand(0, i), 1))
        halves((depth_half, 1))

    @pl.when((step > 0) & (step < strips))
    def _():
        halves((windows_half, 1), (depth_half, 3))

    @pl.when(step == strips)
    def _():
        halves((windows_half, 1))

    @pl.when(step < strips - 1)
    def _():
        halves((project, 1), (expand_half, 1))

    @pl.when(step == strips - 1)
    def _():
        halves((project, 1))


def grid_kernel(tokens_ref, gain_ref, qkv_ref, wo_ref, out_ref, work, wk):
    wk[...] = turned(qkv_ref[0, :, CH : 2 * CH])

    def norm_step(i, carry):
        at = pl.ds(pl.multiple_of(16 * i, 16), 16)
        y = tokens_ref[at].astype(F32).reshape(256, CH)
        rows = pl.ds(pl.multiple_of(256 * i, 256), 256)
        store_halves(work, rows, normalised(y, gain_ref[1:2]))
        return carry

    lax.fori_loop(0, 16, norm_step, 0)

    def set_step(k, carry):
        ats = [pl.ds(SETS * k + n, 256, stride=16) for n in range(SETS)]
        xns = [load_halves(work, at).astype(BF) for at in ats]
        mixed = grid_mix(xns, wk[...], qkv_ref[0])
        for n in range(SETS):
            store_halves(work, ats[n], nn(mixed[n], wo_ref[0]))
        return carry

    lax.fori_loop(0, 16 // SETS, set_step, 0)

    def add_step(i, carry):
        at = pl.ds(pl.multiple_of(16 * i, 16), 16)
        y = load_halves(work, pl.ds(pl.multiple_of(256 * i, 256), 256)).reshape(16, 16, CH)
        out_ref[at] = (tokens_ref[at].astype(F32) + y).astype(BF)
        return carry

    lax.fori_loop(0, 16, add_step, 0)


def whole(shape):
    return pl.BlockSpec(shape, lambda i: (0,) * len(shape))


def layer(shape, n):
    return pl.BlockSpec((1,) + shape[1:], lambda i: (n,) + (0,) * (len(shape) - 1))


def front(edge, image, above, below, sides, params):
    rows_dev, cols_dev, chans = image.shape
    strips = rows_dev // WINDOW
    args = (image, above, below, sides) + params
    return pl.pallas_call(
        front_kernel,
        grid=(strips + 1,),
        in_specs=[pl.BlockSpec(memory_space=pltpu.SMEM)]
        + [whole(a.shape) for a in args[:-2]]
        + [layer(a.shape, 0) for a in args[-2:]],
        out_specs=pl.BlockSpec(
            (1, 8, 4, 2, 16, chans), lambda i: (jnp.maximum(i - 1, 0), 0, 0, 0, 0, 0)
        ),
        out_shape=jax.ShapeDtypeStruct((strips, 8, 4, 2, 16, chans), BF),
        scratch_shapes=[
            pltpu.VMEM((2, 4 * cols_dev, 128), F32),
            pltpu.VMEM((HID // 128, rows_dev + 2, WINDOW + 2, 16, 128), F32),
            pltpu.VMEM((80, HID), F32),
            pltpu.VMEM((WINDOW * cols_dev, HID), BF),
            pltpu.VMEM((2, WINDOW * cols_dev, 128), F32),
            pltpu.VMEM((CH, CH), BF),
            pltpu.VMEM((80, HID), F32),
        ],
        compiler_params=pltpu.CompilerParams(
            dimension_semantics=("arbitrary",), vmem_limit_bytes=48 * 2**20
        ),
        name="front",
    )(edge, *args)


def grid_attention(tokens, gain, qkv, wo):
    return pl.pallas_call(
        grid_kernel,
        grid=(1,),
        in_specs=[whole(tokens.shape), whole(gain.shape), layer(qkv.shape, 1), layer(wo.shape, 1)],
        out_specs=whole(tokens.shape),
        out_shape=jax.ShapeDtypeStruct(tokens.shape, BF),
        scratch_shapes=[
            pltpu.VMEM((2, tokens.shape[0] * tokens.shape[1], 128), F32),
            pltpu.VMEM((CH, CH), BF),
        ],
        compiler_params=pltpu.CompilerParams(
            dimension_semantics=("arbitrary",), vmem_limit_bytes=40 * 2**20
        ),
        name="grid_attention",
    )(tokens, gain, qkv, wo)


def halos(image):
    rows = lax.axis_size("row")
    cols = lax.axis_size("col")
    up = [(i, i + 1) for i in range(rows - 1)]
    down = [(i + 1, i) for i in range(rows - 1)]
    above = lax.ppermute(image[-1:], "row", up)
    below = lax.ppermute(image[:1], "row", down)
    first = jnp.concatenate([above[:, :1], image[:, :1], below[:, :1]], axis=0)[:, 0]
    last = jnp.concatenate([above[:, -1:], image[:, -1:], below[:, -1:]], axis=0)[:, 0]
    left = lax.ppermute(last, "col", [(i, i + 1) for i in range(cols - 1)])
    right = lax.ppermute(first, "col", [(i + 1, i) for i in range(cols - 1)])
    pad = ((0, 40 - left.shape[0]), (0, 0))
    sides = jnp.concatenate([jnp.pad(left, pad), jnp.pad(right, pad)], axis=0)
    return above[0], below[0], sides


def per_device(
    image,
    bn_gain,
    bn_shift,
    expand_weight,
    expand_bias,
    depth_kernel,
    depth_bias,
    project_weight,
    norm_gain,
    qkv_weight,
    out_weight,
):
    rows_dev, cols_dev, chans = image.shape
    row_at = lax.axis_index("row")
    col_at = lax.axis_index("col")
    edge = jnp.stack(
        [
            row_at > 0,
            row_at < lax.axis_size("row") - 1,
            col_at > 0,
            col_at < lax.axis_size("col") - 1,
        ]
    ).astype(jnp.int32)
    above, below, sides = halos(image)
    params = (
        bn_gain[None],
        bn_shift[None],
        expand_weight,
        expand_bias[None],
        depth_kernel,
        depth_bias[None],
        project_weight,
        norm_gain,
        qkv_weight,
        out_weight,
    )
    after_block = front(edge, image, above, below, sides, params)
    outgoing = after_block.reshape(128, 32, chans)
    received = lax.all_to_all(outgoing, ("row", "col"), split_axis=0, concat_axis=0, tiled=True)
    done = grid_attention(received.reshape(256, 16, chans), norm_gain, qkv_weight, out_weight)
    returned = lax.all_to_all(
        done.reshape(128, 32, chans), ("row", "col"), split_axis=0, concat_axis=0, tiled=True
    )
    placed = returned.reshape(4, 8, 4, 2, 2, 8, chans).transpose(0, 2, 4, 3, 1, 5, 6)
    return placed.reshape(rows_dev, cols_dev, chans)


def solution(mesh):
    in_specs = (P("row", "col", None), P(), P(), P(), P(), P(), P(), P(), P(), P(), P())
    out_specs = P("row", "col", None)
    return jax.shard_map(
        per_device, mesh=mesh, in_specs=in_specs, out_specs=out_specs, check_vma=False
    )
```

time: 205 us -> 161 us (0.79)
  Pallas kernels: 104 us -> 53.6 us
  blocking collectives: 34.6 us -> 78.2 us
  waiting for transfers between devices: 29.3 us -> 4.03 us
  starting transfers between devices: 27.6 us -> 11.8 us
  local copies, waits for them, and re-layouts: 6.27 us -> 12.1 us
    pallas_call x2, Pallas kernels: 104 us -> 53.6 us  [the longest x1 35.4 us: front(): pl.pallas_call(front_kernel, grid=(strips + 1,), in_specs=[pl.BlockSpec(m...]
    all_to_all x0 -> x1, blocking collectives: none -> 43.7 us  [per_device(): lax.all_to_all(outgoing, ('row', 'col'), split_axis=0, concat_axis=0, til...]
    all_to_all x1 -> x0, waiting for transfers between devices: 28.6 us -> none  [per_device(): lax.all_to_all(outgoing, ('row', 'col'), split_axis=0, concat_axis=0, til...]
    all_to_all x1 -> x0, starting transfers between devices: 15.9 us -> none  [per_device(): lax.all_to_all(outgoing, ('row', 'col'), split_axis=0, concat_axis=0, til...]
    unnamed x20 -> x26, local copies, waits for them, and re-layouts: 0.62 us -> 8.55 us
    ppermute x1, waiting for transfers between devices: 0.01 us -> 3.26 us  [halos(): below = lax.ppermute(image[:1], 'row', down)]
  transfers between devices with their start and end apart: 5 -> 4, of which waited for: 2 -> 2; matrix products, arithmetic and copies ran while one was open for 3% -> 1% of each run, Pallas kernels for 0% -> 0%
where the time goes in v2:
time: 161 us; the launch traced here: 160 us
  blocking collectives  78.2 us (49%)
  Pallas kernels  53.6 us (33%)
  local copies, waits for them, and re-layouts  12.1 us (8%)
  starting transfers between devices  11.8 us (7%)
  waiting for transfers between devices  4.03 us (3%)
    all_to_all x1, blocking collectives, per_device(): lax.all_to_all(outgoing, ('row', 'col'), split_axis=0, concat_axis=0, til...  43.7 us
    pallas_call x1, Pallas kernels, front(): pl.pallas_call(front_kernel, grid=(strips + 1,), in_specs=[pl.BlockSpec(m...  35.4 us
    all_to_all x1, blocking collectives, per_device(): lax.all_to_all(done.reshape(128, 32, chans), ('row', 'col'), split_axis=0...  34.6 us
    pallas_call x1, Pallas kernels, grid_attention(): pl.pallas_call(grid_kernel, grid=(1,), in_specs=[whole(tokens.shape), who...  18.3 us
    unnamed x26, local copies, waits for them, and re-layouts  8.55 us
    ppermute x1, starting transfers between devices, halos(): above = lax.ppermute(image[-1:], 'row', up)  4.59 us
    ppermute x1, starting transfers between devices, halos(): left = lax.ppermute(last, 'col', [(i, i + 1) for i in range(cols - 1)])  3.99 us
    ppermute x1, waiting for transfers between devices, halos(): below = lax.ppermute(image[:1], 'row', down)  3.26 us
  transfers between devices with their start and end apart: 4, of which 2 were waited for; matrix products, arithmetic and copies ran while one was open for 1% of the time, Pallas kernels for 0%

profile of v2, /device:TPU:1, one launch (start us, length us, event | category | flops | bytes accessed | tf_op | source)
XLA Modules:
  0.0 160.0 jit_solution(10206110923944692939)
XLA Ops:
  0.0 0.9 fusion.4
  0.9 0.1 copy.24
  1.0 4.6 %collective-permute-start = (bf16[1,128,256]{2,0,1:T(2,128)(2,1)S(1)}, bf16[1,128,256]{2,0,1:T(2,128)(2,1)S(1)}, u32[]{:S(2)}, u32[]{:S(2)}) collective-permute-start(bf16[1,128,256]{2,0,1:T(2,128)(2,1)S(1)} %copy.24), channel_id=1, source_target_pairs={{0,8},{8,16},{16,24},{24,32},{32,40},{40,48},{48,56},{56,64},{64,7... | collective-permute-start | bytes 196616 | tf_op jit(solution)/shard_map/ppermute | solution.py:445
  5.6 0.1 copy.25
  5.7 1.9 %collective-permute-start.1 = (bf16[1,128,256]{2,0,1:T(2,128)(2,1)S(1)}, bf16[1,128,256]{2,0,1:T(2,128)(2,1)S(1)}, u32[]{:S(2)}, u32[]{:S(2)}) collective-permute-start(bf16[1,128,256]{2,0,1:T(2,128)(2,1)S(1)} %copy.25), channel_id=1, source_target_pairs={{8,0},{16,8},{24,16},{32,24},{40,32},{48,40},{56,48},{64,56},{72,6... | collective-permute-start | bytes 196616 | tf_op jit(solution)/shard_map/ppermute | solution.py:446
  7.6 1.0 fusion.3
  8.7 0.0 collective-permute-done
  8.7 3.3 %collective-permute-done.1 = bf16[1,128,256]{2,0,1:T(2,128)(2,1)S(1)} collective-permute-done((bf16[1,128,256]{2,0,1:T(2,128)(2,1)S(1)}, bf16[1,128,256]{2,0,1:T(2,128)(2,1)S(1)}, u32[]{:S(2)}, u32[]{:S(2)}) %collective-permute-start.1) | collective-permute-done | bytes 65568 | tf_op jit(solution)/shard_map/ppermute | solution.py:446
  12.0 1.3 collective-permute-start.3
  13.3 4.0 %collective-permute-start.2 = (bf16[34,256]{1,0:T(8,128)(2,1)S(1)}, bf16[34,256]{1,0:T(8,128)(2,1)S(1)}, u32[]{:S(2)}, u32[]{:S(2)}) collective-permute-start(bf16[34,256]{1,0:T(8,128)(2,1)S(1)} %maximum_bitcast_fusion), channel_id=1, source_target_pairs={{0,1},{1,2},{2,3},{3,4},{4,5},{5,6},{6,7},{8,9},{9,10},{10,11},{11... | collective-permute-start | bytes 52232 | tf_op jit(solution)/shard_map/ppermute | solution.py:449
  17.3 0.1 add_convert_fusion.edge_ref
  17.4 0.0 collective-permute-done.3
  17.5 0.8 collective-permute-done.2
  18.2 0.0 copy-start
  18.2 1.1 copy-done
  19.4 0.0 copy-start.1
  19.4 0.9 copy-done.1
  20.3 0.0 copy-start.2
  20.3 1.0 copy-done.2
  21.4 0.0 copy-start.3
  21.4 1.0 copy-done.3
  22.4 0.7 copy-done.4
  23.1 0.7 copy-done.5
  23.8 0.7 copy-done.6
  24.5 0.7 copy-done.7
  25.2 0.7 copy-done.8
  25.9 0.7 copy-done.9
  26.5 35.4 %front.1 = bf16[4,8,4,2,16,256]{5,4,3,2,1,0:T(8,128)(2,1)S(1)} custom-call(s32[4]{0:T(128)S(1)} %add_convert_fusion.edge_ref, bf16[32,128,256]{2,1,0:T(8,128)(2,1)} %image_ref.1, bf16[128,256]{1,0:T(8,128)(2,1)S(1)} %bitcast.28, bf16[128,256]{1,0:T(8,128)(2,1)S(1)} %bitcast.29, bf16[80,256]{1,0:T(8,128)(2,1)S(1)} %fusion.2.sides_ref, f32[1,256]{1,0:T(1,128)S(1)} %bitcast.32, ...), custom_call_target="tpu_custom_call" | custom-call | tf_op jit(solution)/shard_map/front/pallas_call | solution.py:396
  61.9 43.7 %all_to_all.10 = bf16[128,32,256]{2,1,0:T(8,128)(2,1)S(1)} all-to-all(bf16[128,32,256]{2,1,0:T(8,128)(2,1)S(1)} %bitcast.27), channel_id=1, replica_groups=mesh['row'=16,'col'=8] {'row','col'}, dimensions={0} | all-to-all | bytes 4194304 | tf_op jit(solution)/shard_map/all_to_all | solution.py:495
  105.6 18.3 %grid_attention.1 = bf16[256,16,256]{2,1,0:T(8,128)(2,1)S(1)} custom-call(bf16[256,16,256]{2,1,0:T(8,128)(2,1)S(1)} %bitcast.25, f32[2,256]{1,0:T(2,128)S(1)} %copy-done.5, bf16[2,256,768]{2,1,0:T(8,128)(2,1)S(1)} %copy-done, bf16[2,256,256]{2,1,0:T(8,128)(2,1)S(1)} %copy-done.1), custom_call_target="tpu_custom_call" | custom-call | tf_op jit(solution)/shard_map/grid_attention/pallas_call | solution.py:423
  123.9 34.6 %all_to_all.11 = bf16[128,32,256]{2,1,0:T(8,128)(2,1)S(1)} all-to-all(bf16[128,32,256]{2,1,0:T(8,128)(2,1)S(1)} %bitcast.26), channel_id=1, replica_groups=mesh['row'=16,'col'=8] {'row','col'}, dimensions={0} | all-to-all | bytes 4194304 | tf_op jit(solution)/shard_map/all_to_all | solution.py:497
  158.4 1.6 %copy.21 = bf16[4,8,4,2,2,8,256]{6,5,1,3,4,2,0:T(8,128)(2,1)} copy(bf16[4,8,4,2,2,8,256]{6,5,4,3,2,1,0:T(8,128)(2,1)S(1)} %bitcast.34) | data formatting | bytes 4194304 | tf_op jit(solution)/shard_map/reshape | solution.py:500
  (15 shorter events, 0.1 us)
Async XLA Ops:
  1.0 7.7 %collective-permute-start = (bf16[1,128,256]{2,0,1:T(2,128)(2,1)S(1)}, bf16[1,128,256]{2,0,1:T(2,128)(2,1)S(1)}, u32[]{:S(2)}, u32[]{:S(2)}) collective-permute-start(bf16[1,128,256]{2,0,1:T(2,128)(2,1)S(1)} %copy.24), channel_id=1, source_target_pairs={{0,8},{8,16},{16,24},{24,32},{32,40},{40,48},{48,56},{56,64},{64,7... | collective-permute-start | bytes 196616 | tf_op jit(solution)/shard_map/ppermute | solution.py:445
  5.7 6.3 %collective-permute-start.1 = (bf16[1,128,256]{2,0,1:T(2,128)(2,1)S(1)}, bf16[1,128,256]{2,0,1:T(2,128)(2,1)S(1)}, u32[]{:S(2)}, u32[]{:S(2)}) collective-permute-start(bf16[1,128,256]{2,0,1:T(2,128)(2,1)S(1)} %copy.25), channel_id=1, source_target_pairs={{8,0},{16,8},{24,16},{32,24},{40,32},{48,40},{56,48},{64,56},{72,6... | collective-permute-start | bytes 196616 | tf_op jit(solution)/shard_map/ppermute | solution.py:446
  12.0 5.4 %collective-permute-start.3 = (bf16[34,256]{1,0:T(8,128)(2,1)S(1)}, bf16[34,256]{1,0:T(8,128)(2,1)S(1)}, u32[]{:S(2)}, u32[]{:S(2)}) collective-permute-start(bf16[34,256]{1,0:T(8,128)(2,1)S(1)} %maximum_bitcast_fusion.1), channel_id=1, source_target_pairs={{1,0},{2,1},{3,2},{4,3},{5,4},{6,5},{7,6},{9,8},{10,9},{11,10},{12... | collective-permute-start | bytes 52232 | tf_op jit(solution)/shard_map/ppermute | solution.py:450
  13.3 4.9 %collective-permute-start.2 = (bf16[34,256]{1,0:T(8,128)(2,1)S(1)}, bf16[34,256]{1,0:T(8,128)(2,1)S(1)}, u32[]{:S(2)}, u32[]{:S(2)}) collective-permute-start(bf16[34,256]{1,0:T(8,128)(2,1)S(1)} %maximum_bitcast_fusion), channel_id=1, source_target_pairs={{0,1},{1,2},{2,3},{3,4},{4,5},{5,6},{6,7},{8,9},{9,10},{10,11},{11... | collective-permute-start | bytes 52232 | tf_op jit(solution)/shard_map/ppermute | solution.py:449
  18.2 1.1 copy-start
  19.4 0.9 copy-start.1
  20.3 1.0 copy-start.2
  21.4 1.0 copy-start.3
  22.4 0.7 copy-start.4
  23.1 0.7 copy-start.5
  23.8 0.7 copy-start.6
  24.5 0.7 copy-start.7
  25.2 0.7 copy-start.8
  25.9 0.7 copy-start.9

commit v3 on v2

--- a/solution.py
+++ b/solution.py
@@ -353,32 +353,31 @@
 def grid_kernel(tokens_ref, gain_ref, qkv_ref, wo_ref, out_ref, work, wk):
     wk[...] = turned(qkv_ref[0, :, CH : 2 * CH])
 
-    def norm_step(i, carry):
+    def spread_step(i, carry):
         at = pl.ds(pl.multiple_of(16 * i, 16), 16)
         y = tokens_ref[at].astype(F32).reshape(256, CH)
-        rows = pl.ds(pl.multiple_of(256 * i, 256), 256)
-        store_halves(work, rows, normalised(y, gain_ref[1:2]))
+        store_halves(work, pl.ds(pl.multiple_of(256 * i, 256), 256), y)
         return carry
 
-    lax.fori_loop(0, 16, norm_step, 0)
+    lax.fori_loop(0, 16, spread_step, 0)
 
     def set_step(k, carry):
         ats = [pl.ds(SETS * k + n, 256, stride=16) for n in range(SETS)]
-        xns = [load_halves(work, at).astype(BF) for at in ats]
+        xns = [normalised(load_halves(work, at), gain_ref[1:2]).astype(BF) for at in ats]
         mixed = grid_mix(xns, wk[...], qkv_ref[0])
         for n in range(SETS):
-            store_halves(work, ats[n], nn(mixed[n], wo_ref[0]))
+            store_halves(work, ats[n], load_halves(work, ats[n]) + nn(mixed[n], wo_ref[0]))
         return carry
 
     lax.fori_loop(0, 16 // SETS, set_step, 0)
 
-    def add_step(i, carry):
+    def collect_step(i, carry):
         at = pl.ds(pl.multiple_of(16 * i, 16), 16)
-        y = load_halves(work, pl.ds(pl.multiple_of(256 * i, 256), 256)).reshape(16, 16, CH)
-        out_ref[at] = (tokens_ref[at].astype(F32) + y).astype(BF)
+        y = load_halves(work, pl.ds(pl.multiple_of(256 * i, 256), 256))
+        out_ref[at] = y.reshape(16, 16, CH).astype(BF)
         return carry
 
-    lax.fori_loop(0, 16, add_step, 0)
+    lax.fori_loop(0, 16, collect_step, 0)
 
 
 def whole(shape):
@@ -413,7 +412,7 @@
             pltpu.VMEM((80, HID), F32),
         ],
         compiler_params=pltpu.CompilerParams(
-            dimension_semantics=("arbitrary",), vmem_limit_bytes=48 * 2**20
+            dimension_semantics=("arbitrary",), vmem_limit_bytes=60 * 2**20
         ),
         name="front",
     )(edge, *args)

time: 161 us -> 153 us (0.950)
  local copies, waits for them, and re-layouts: 12.1 us -> 5.01 us
    unnamed x26 -> x12, local copies, waits for them, and re-layouts: 8.55 us -> 1.49 us
  transfers between devices with their start and end apart: 4 -> 4, of which waited for: 2 -> 1; matrix products, arithmetic and copies ran while one was open for 1% -> 2% of each run, Pallas kernels for 0% -> 0%
where the time goes in v3:
time: 153 us
  blocking collectives  77.5 us (51%)
  Pallas kernels  53.8 us (35%)
  starting transfers between devices  11.8 us (8%)
  local copies, waits for them, and re-layouts  5.01 us (3%)
  waiting for transfers between devices  3.27 us (2%)
    all_to_all x1, blocking collectives, per_device(): lax.all_to_all(outgoing, ('row', 'col'), split_axis=0, concat_axis=0, til...  42.9 us
    pallas_call x1, Pallas kernels, front(): pl.pallas_call(front_kernel, grid=(strips + 1,), in_specs=[pl.BlockSpec(m...  36.5 us
    all_to_all x1, blocking collectives, per_device(): lax.all_to_all(done.reshape(128, 32, chans), ('row', 'col'), split_axis=0...  34.6 us
    pallas_call x1, Pallas kernels, grid_attention(): pl.pallas_call(grid_kernel, grid=(1,), in_specs=[whole(tokens.shape), who...  17.3 us
    ppermute x1, starting transfers between devices, halos(): above = lax.ppermute(image[-1:], 'row', up)  4.59 us
    ppermute x1, starting transfers between devices, halos(): left = lax.ppermute(last, 'col', [(i, i + 1) for i in range(cols - 1)])  3.99 us
    ppermute x1, waiting for transfers between devices, halos(): below = lax.ppermute(image[:1], 'row', down)  3.26 us
  transfers between devices with their start and end apart: 4, of which 1 were waited for; matrix products, arithmetic and copies ran while one was open for 2% of the time, Pallas kernels for 0%

profile of v3, /device:TPU:1, one launch (start us, length us, event | category | flops | bytes accessed | tf_op | source)
XLA Modules:
  0.0 152.7 jit_solution(8054137914965968884)
XLA Ops:
  0.0 0.9 fusion.4
  0.9 0.1 copy.24
  1.0 4.6 %collective-permute-start = (bf16[1,128,256]{2,0,1:T(2,128)(2,1)S(1)}, bf16[1,128,256]{2,0,1:T(2,128)(2,1)S(1)}, u32[]{:S(2)}, u32[]{:S(2)}) collective-permute-start(bf16[1,128,256]{2,0,1:T(2,128)(2,1)S(1)} %copy.24), channel_id=1, source_target_pairs={{0,8},{8,16},{16,24},{24,32},{32,40},{40,48},{48,56},{56,64},{64,7... | collective-permute-start | bytes 196616 | tf_op jit(solution)/shard_map/ppermute | solution.py:444
  5.6 0.1 copy.25
  5.7 1.9 %collective-permute-start.1 = (bf16[1,128,256]{2,0,1:T(2,128)(2,1)S(1)}, bf16[1,128,256]{2,0,1:T(2,128)(2,1)S(1)}, u32[]{:S(2)}, u32[]{:S(2)}) collective-permute-start(bf16[1,128,256]{2,0,1:T(2,128)(2,1)S(1)} %copy.25), channel_id=1, source_target_pairs={{8,0},{16,8},{24,16},{32,24},{40,32},{48,40},{56,48},{64,56},{72,6... | collective-permute-start | bytes 196616 | tf_op jit(solution)/shard_map/ppermute | solution.py:445
  7.6 1.0 fusion.3
  8.7 0.0 collective-permute-done
  8.7 3.3 %collective-permute-done.1 = bf16[1,128,256]{2,0,1:T(2,128)(2,1)S(1)} collective-permute-done((bf16[1,128,256]{2,0,1:T(2,128)(2,1)S(1)}, bf16[1,128,256]{2,0,1:T(2,128)(2,1)S(1)}, u32[]{:S(2)}, u32[]{:S(2)}) %collective-permute-start.1) | collective-permute-done | bytes 65568 | tf_op jit(solution)/shard_map/ppermute | solution.py:445
  12.0 1.3 collective-permute-start.3
  13.3 4.0 %collective-permute-start.2 = (bf16[34,256]{1,0:T(8,128)(2,1)S(1)}, bf16[34,256]{1,0:T(8,128)(2,1)S(1)}, u32[]{:S(2)}, u32[]{:S(2)}) collective-permute-start(bf16[34,256]{1,0:T(8,128)(2,1)S(1)} %maximum_bitcast_fusion), channel_id=1, source_target_pairs={{0,1},{1,2},{2,3},{3,4},{4,5},{5,6},{6,7},{8,9},{9,10},{10,11},{11... | collective-permute-start | bytes 52232 | tf_op jit(solution)/shard_map/ppermute | solution.py:448
  17.3 0.6 add_convert_fusion.edge_ref
  17.9 0.6 copy.31
  18.6 0.6 copy.30
  19.2 0.0 collective-permute-done.3
  19.2 0.0 collective-permute-done.2
  19.2 0.6 fusion.2.sides_ref
  19.8 36.5 %front.1 = bf16[4,8,4,2,16,256]{5,4,3,2,1,0:T(8,128)(2,1)} custom-call(s32[4]{0:T(128)} %add_convert_fusion.edge_ref, bf16[32,128,256]{2,1,0:T(8,128)(2,1)} %image_ref.1, bf16[128,256]{1,0:T(8,128)(2,1)} %bitcast.29, bf16[128,256]{1,0:T(8,128)(2,1)} %bitcast.30, bf16[80,256]{1,0:T(8,128)(2,1)} %fusion.2.sides_ref, f32[1,256]{1,0:T(1,128)} %bitcast.33, ...), custom_call_target="tpu_custom_call" | custom-call | tf_op jit(solution)/shard_map/front/pallas_call | solution.py:395
  56.3 0.0 copy-start
  56.3 0.0 copy-start.1
  56.3 0.0 copy-start.2
  56.4 42.9 %all_to_all.10 = bf16[128,32,256]{2,1,0:T(8,128)(2,1)S(1)} all-to-all(bf16[128,32,256]{2,1,0:T(8,128)(2,1)} %bitcast.27), channel_id=1, replica_groups=mesh['row'=16,'col'=8] {'row','col'}, dimensions={0} | all-to-all | bytes 4194304 | tf_op jit(solution)/shard_map/all_to_all | solution.py:494
  99.2 0.0 copy-done
  99.2 0.0 copy-done.1
  99.2 0.0 copy-done.2
  99.2 17.3 %grid_attention.1 = bf16[256,16,256]{2,1,0:T(8,128)(2,1)S(1)} custom-call(bf16[256,16,256]{2,1,0:T(8,128)(2,1)S(1)} %bitcast.25, f32[2,256]{1,0:T(2,128)S(1)} %copy-done.2, bf16[2,256,768]{2,1,0:T(8,128)(2,1)S(1)} %copy-done, bf16[2,256,256]{2,1,0:T(8,128)(2,1)S(1)} %copy-done.1), custom_call_target="tpu_custom_call" | custom-call | tf_op jit(solution)/shard_map/grid_attention/pallas_call | solution.py:422
  116.5 34.6 %all_to_all.11 = bf16[128,32,256]{2,1,0:T(8,128)(2,1)S(1)} all-to-all(bf16[128,32,256]{2,1,0:T(8,128)(2,1)S(1)} %bitcast.26), channel_id=1, replica_groups=mesh['row'=16,'col'=8] {'row','col'}, dimensions={0} | all-to-all | bytes 4194304 | tf_op jit(solution)/shard_map/all_to_all | solution.py:496
  151.1 1.6 %copy.21 = bf16[4,8,4,2,2,8,256]{6,5,1,3,4,2,0:T(8,128)(2,1)} copy(bf16[4,8,4,2,2,8,256]{6,5,4,3,2,1,0:T(8,128)(2,1)S(1)} %bitcast.28) | data formatting | bytes 4194304 | tf_op jit(solution)/shard_map/reshape | solution.py:499
  (6 shorter events, 0.0 us)
Async XLA Ops:
  1.0 7.7 %collective-permute-start = (bf16[1,128,256]{2,0,1:T(2,128)(2,1)S(1)}, bf16[1,128,256]{2,0,1:T(2,128)(2,1)S(1)}, u32[]{:S(2)}, u32[]{:S(2)}) collective-permute-start(bf16[1,128,256]{2,0,1:T(2,128)(2,1)S(1)} %copy.24), channel_id=1, source_target_pairs={{0,8},{8,16},{16,24},{24,32},{32,40},{40,48},{48,56},{56,64},{64,7... | collective-permute-start | bytes 196616 | tf_op jit(solution)/shard_map/ppermute | solution.py:444
  5.7 6.3 %collective-permute-start.1 = (bf16[1,128,256]{2,0,1:T(2,128)(2,1)S(1)}, bf16[1,128,256]{2,0,1:T(2,128)(2,1)S(1)}, u32[]{:S(2)}, u32[]{:S(2)}) collective-permute-start(bf16[1,128,256]{2,0,1:T(2,128)(2,1)S(1)} %copy.25), channel_id=1, source_target_pairs={{8,0},{16,8},{24,16},{32,24},{40,32},{48,40},{56,48},{64,56},{72,6... | collective-permute-start | bytes 196616 | tf_op jit(solution)/shard_map/ppermute | solution.py:445
  12.0 7.2 %collective-permute-start.3 = (bf16[34,256]{1,0:T(8,128)(2,1)S(1)}, bf16[34,256]{1,0:T(8,128)(2,1)S(1)}, u32[]{:S(2)}, u32[]{:S(2)}) collective-permute-start(bf16[34,256]{1,0:T(8,128)(2,1)S(1)} %maximum_bitcast_fusion.1), channel_id=1, source_target_pairs={{1,0},{2,1},{3,2},{4,3},{5,4},{6,5},{7,6},{9,8},{10,9},{11,10},{12... | collective-permute-start | bytes 52232 | tf_op jit(solution)/shard_map/ppermute | solution.py:449
  13.3 5.9 %collective-permute-start.2 = (bf16[34,256]{1,0:T(8,128)(2,1)S(1)}, bf16[34,256]{1,0:T(8,128)(2,1)S(1)}, u32[]{:S(2)}, u32[]{:S(2)}) collective-permute-start(bf16[34,256]{1,0:T(8,128)(2,1)S(1)} %maximum_bitcast_fusion), channel_id=1, source_target_pairs={{0,1},{1,2},{2,3},{3,4},{4,5},{5,6},{6,7},{8,9},{9,10},{10,11},{11... | collective-permute-start | bytes 52232 | tf_op jit(solution)/shard_map/ppermute | solution.py:448
  56.3 42.9 %copy-start = (bf16[2,256,768]{2,1,0:T(8,128)(2,1)S(1)}, bf16[2,256,768]{2,1,0:T(8,128)(2,1)}, u32[]{:S(2)}) copy-start(bf16[2,256,768]{2,1,0:T(8,128)(2,1)} %qkv_ref.3) | copy-start | bytes 2359300
  56.3 42.9 %copy-start.1 = (bf16[2,256,256]{2,1,0:T(8,128)(2,1)S(1)}, bf16[2,256,256]{2,1,0:T(8,128)(2,1)}, u32[]{:S(2)}) copy-start(bf16[2,256,256]{2,1,0:T(8,128)(2,1)} %wo_ref.3) | copy-start | bytes 786436
  56.3 42.9 %copy-start.2 = (f32[2,256]{1,0:T(2,128)S(1)}, f32[2,256]{1,0:T(2,128)}, u32[]{:S(2)}) copy-start(f32[2,256]{1,0:T(2,128)} %gain_ref.3) | copy-start | bytes 6148

commit v4 on v3

--- a/solution.py
+++ b/solution.py
@@ -179,7 +179,8 @@
     image_ref,
     above_ref,
     below_ref,
-    sides_ref,
+    left_ref,
+    right_ref,
     bn_gain_ref,
     bn_shift_ref,
     expand_ref,
@@ -250,7 +251,7 @@
             row = depth_ref[tap // 3, tap % 3 : tap % 3 + 1].astype(F32) * 0.5
             taps[8 * tap : 8 * tap + 8, :] = jnp.broadcast_to(row, (8, HID))
         taps[72:80, :] = jnp.broadcast_to(depth_bias_ref[...] * CUBE, (8, HID))
-        cells = normed(sides_ref[...]).astype(BF)
+        cells = jnp.concatenate([normed(left_ref[...]), normed(right_ref[...])], axis=0).astype(BF)
         index = lax.broadcasted_iota(jnp.int32, (80, 1), 0)
         right = index >= 40
         row = jnp.where(right, index - 40, index)
@@ -388,10 +389,10 @@
     return pl.BlockSpec((1,) + shape[1:], lambda i: (n,) + (0,) * (len(shape) - 1))
 
 
-def front(edge, image, above, below, sides, params):
+def front(edge, image, above, below, left, right, params):
     rows_dev, cols_dev, chans = image.shape
     strips = rows_dev // WINDOW
-    args = (image, above, below, sides) + params
+    args = (image, above, below, left, right) + params
     return pl.pallas_call(
         front_kernel,
         grid=(strips + 1,),
@@ -439,17 +440,14 @@
 def halos(image):
     rows = lax.axis_size("row")
     cols = lax.axis_size("col")
-    up = [(i, i + 1) for i in range(rows - 1)]
-    down = [(i + 1, i) for i in range(rows - 1)]
-    above = lax.ppermute(image[-1:], "row", up)
-    below = lax.ppermute(image[:1], "row", down)
-    first = jnp.concatenate([above[:, :1], image[:, :1], below[:, :1]], axis=0)[:, 0]
-    last = jnp.concatenate([above[:, -1:], image[:, -1:], below[:, -1:]], axis=0)[:, 0]
+    above = lax.ppermute(image[-1], "row", [(i, i + 1) for i in range(rows - 1)])
+    below = lax.ppermute(image[0], "row", [(i + 1, i) for i in range(rows - 1)])
+    none = jnp.zeros((38 - image.shape[0], image.shape[2]), image.dtype)
+    first = jnp.concatenate([above[:1], image[:, 0], below[:1], none], axis=0)
+    last = jnp.concatenate([above[-1:], image[:, -1], below[-1:], none], axis=0)
     left = lax.ppermute(last, "col", [(i, i + 1) for i in range(cols - 1)])
     right = lax.ppermute(first, "col", [(i + 1, i) for i in range(cols - 1)])
-    pad = ((0, 40 - left.shape[0]), (0, 0))
-    sides = jnp.concatenate([jnp.pad(left, pad), jnp.pad(right, pad)], axis=0)
-    return above[0], below[0], sides
+    return above, below, left, right
 
 
 def per_device(
@@ -476,7 +474,7 @@
             col_at < lax.axis_size("col") - 1,
         ]
     ).astype(jnp.int32)
-    above, below, sides = halos(image)
+    above, below, left, right = halos(image)
     params = (
         bn_gain[None],
         bn_shift[None],
@@ -489,7 +487,7 @@
         qkv_weight,
         out_weight,
     )
-    after_block = front(edge, image, above, below, sides, params)
+    after_block = front(edge, image, above, below, left, right, params)
     outgoing = after_block.reshape(128, 32, chans)
     received = lax.all_to_all(outgoing, ("row", "col"), split_axis=0, concat_axis=0, tiled=True)
     done = grid_attention(received.reshape(256, 16, chans), norm_gain, qkv_weight, out_weight)

time: 153 us -> 153 us (level)
  blocking collectives: 77.5 us -> 81.5 us
  waiting for transfers between devices: 3.27 us -> 0.37 us
    all_to_all x1, blocking collectives: 42.9 us -> 47 us  [per_device(): lax.all_to_all(outgoing, ('row', 'col'), split_axis=0, concat_axis=0, til...]
    ppermute x2, waiting for transfers between devices: 3.27 us -> 0.15 us  [the longest x1 0.15 us: halos(): lax.ppermute(image[-1], 'row', [(i, i + 1) for i in range(rows - 1)])]
  transfers between devices with their start and end apart: 4 -> 4, of which waited for: 1 -> 2; matrix products, arithmetic and copies ran while one was open for 2% -> 1% of each run, Pallas kernels for 0% -> 0%
where the time goes in v4:
time: 153 us
  blocking collectives  81.5 us (53%)
  Pallas kernels  53.8 us (35%)
  starting transfers between devices  11.8 us (8%)
  local copies, waits for them, and re-layouts  4.23 us (3%)
    all_to_all x1, blocking collectives, per_device(): lax.all_to_all(outgoing, ('row', 'col'), split_axis=0, concat_axis=0, til...  47 us
    pallas_call x1, Pallas kernels, front(): pl.pallas_call(front_kernel, grid=(strips + 1,), in_specs=[pl.BlockSpec(m...  36.5 us
    all_to_all x1, blocking collectives, per_device(): lax.all_to_all(done.reshape(128, 32, chans), ('row', 'col'), split_axis=0...  34.6 us
    pallas_call x1, Pallas kernels, grid_attention(): pl.pallas_call(grid_kernel, grid=(1,), in_specs=[whole(tokens.shape), who...  17.3 us
    ppermute x1, starting transfers between devices, halos(): left = lax.ppermute(last, 'col', [(i, i + 1) for i in range(cols - 1)])  3.99 us
    ppermute x1, starting transfers between devices, halos(): below = lax.ppermute(image[0], 'row', [(i + 1, i) for i in range(rows - 1)])  3.33 us
    ppermute x1, starting transfers between devices, halos(): lax.ppermute(image[-1], 'row', [(i, i + 1) for i in range(rows - 1)])  3.19 us
  transfers between devices with their start and end apart: 4, of which 2 were waited for; matrix products, arithmetic and copies ran while one was open for 1% of the time, Pallas kernels for 0%

profile of v4, /device:TPU:1, one launch (start us, length us, event | category | flops | bytes accessed | tf_op | source)
XLA Modules:
  0.0 152.5 jit_solution(5812304575122270676)
XLA Ops:
  0.0 0.9 slice_bitcast_fusion
  0.9 3.3 %collective-permute-start.1 = (bf16[128,256]{1,0:T(8,128)(2,1)S(1)}, bf16[128,256]{1,0:T(8,128)(2,1)S(1)}, u32[]{:S(2)}, u32[]{:S(2)}) collective-permute-start(bf16[128,256]{1,0:T(8,128)(2,1)S(1)} %get-tuple-element.7), channel_id=1, source_target_pairs={{8,0},{16,8},{24,16},{32,24},{40,32},{48,40},{56,48},{64,56},{72,6... | collective-permute-start | bytes 196616 | tf_op jit(solution)/shard_map/ppermute | solution.py:444
  4.2 3.2 %collective-permute-start = (bf16[128,256]{1,0:T(8,128)(2,1)S(1)}, bf16[128,256]{1,0:T(8,128)(2,1)S(1)}, u32[]{:S(2)}, u32[]{:S(2)}) collective-permute-start(bf16[128,256]{1,0:T(8,128)(2,1)S(1)} %get-tuple-element.8), channel_id=1, source_target_pairs={{0,8},{8,16},{16,24},{24,32},{32,40},{40,48},{48,56},{56,64},{64,7... | collective-permute-start | bytes 196616 | tf_op jit(solution)/shard_map/ppermute | solution.py:443
  7.4 1.0 fusion
  8.5 0.1 pad.7.clone
  8.6 0.0 collective-permute-done.1.below_ref
  8.6 0.0 copy-start.3
  8.6 0.2 collective-permute-done.above_ref
  8.7 0.0 copy-start.4
  8.7 0.1 maximum_maximum_fusion.1
  8.8 1.3 collective-permute-start.3
  10.1 4.0 %collective-permute-start.2 = (bf16[40,256]{1,0:T(8,128)(2,1)S(1)}, bf16[40,256]{1,0:T(8,128)(2,1)S(1)}, u32[]{:S(2)}, u32[]{:S(2)}) collective-permute-start(bf16[40,256]{1,0:T(8,128)(2,1)S(1)} %get-tuple-element.14), channel_id=1, source_target_pairs={{0,1},{1,2},{2,3},{3,4},{4,5},{5,6},{6,7},{8,9},{9,10},{10,11},{11... | collective-permute-start | bytes 61448 | tf_op jit(solution)/shard_map/ppermute | solution.py:448
  14.1 0.7 add_convert_fusion.edge_ref
  14.8 0.0 collective-permute-done.3.right_ref
  14.8 0.0 copy-start.5
  14.8 0.2 collective-permute-done.2.left_ref
  15.0 0.0 copy-start.6
  15.0 0.0 copy-done.3
  15.0 0.0 copy-done.4
  15.0 0.4 copy-done.5
  15.4 0.2 copy-done.6
  15.6 36.5 %front.1 = bf16[4,8,4,2,16,256]{5,4,3,2,1,0:T(8,128)(2,1)} custom-call(s32[4]{0:T(128)} %add_convert_fusion.edge_ref, bf16[32,128,256]{2,1,0:T(8,128)(2,1)} %image_ref.1, bf16[128,256]{1,0:T(8,128)(2,1)} %copy-done.4, bf16[128,256]{1,0:T(8,128)(2,1)} %copy-done.3, bf16[40,256]{1,0:T(8,128)(2,1)} %copy-done.6, bf16[40,256]{1,0:T(8,128)(2,1)} %copy-done.5, ...), custom_call_target="tpu_custom_call" | custom-call | tf_op jit(solution)/shard_map/front/pallas_call | solution.py:396
  52.1 0.0 copy-start
  52.1 0.0 copy-start.1
  52.1 0.0 copy-start.2
  52.1 47.0 %all_to_all.10 = bf16[128,32,256]{2,1,0:T(8,128)(2,1)S(1)} all-to-all(bf16[128,32,256]{2,1,0:T(8,128)(2,1)} %bitcast.25), channel_id=1, replica_groups=mesh['row'=16,'col'=8] {'row','col'}, dimensions={0} | all-to-all | bytes 4194304 | tf_op jit(solution)/shard_map/all_to_all | solution.py:492
  99.1 0.0 copy-done
  99.1 0.0 copy-done.1
  99.1 0.0 copy-done.2
  99.1 17.3 %grid_attention.1 = bf16[256,16,256]{2,1,0:T(8,128)(2,1)S(1)} custom-call(bf16[256,16,256]{2,1,0:T(8,128)(2,1)S(1)} %bitcast.23, f32[2,256]{1,0:T(2,128)S(1)} %copy-done.2, bf16[2,256,768]{2,1,0:T(8,128)(2,1)S(1)} %copy-done, bf16[2,256,256]{2,1,0:T(8,128)(2,1)S(1)} %copy-done.1), custom_call_target="tpu_custom_call" | custom-call | tf_op jit(solution)/shard_map/grid_attention/pallas_call | solution.py:423
  116.3 34.6 %all_to_all.11 = bf16[128,32,256]{2,1,0:T(8,128)(2,1)S(1)} all-to-all(bf16[128,32,256]{2,1,0:T(8,128)(2,1)S(1)} %bitcast.24), channel_id=1, replica_groups=mesh['row'=16,'col'=8] {'row','col'}, dimensions={0} | all-to-all | bytes 4194304 | tf_op jit(solution)/shard_map/all_to_all | solution.py:494
  150.9 1.6 %copy.14 = bf16[4,8,4,2,2,8,256]{6,5,1,3,4,2,0:T(8,128)(2,1)} copy(bf16[4,8,4,2,2,8,256]{6,5,4,3,2,1,0:T(8,128)(2,1)S(1)} %bitcast.26) | data formatting | bytes 4194304 | tf_op jit(solution)/shard_map/reshape | solution.py:497
  (4 shorter events, 0.0 us)
Async XLA Ops:
  0.9 7.7 %collective-permute-start.1 = (bf16[128,256]{1,0:T(8,128)(2,1)S(1)}, bf16[128,256]{1,0:T(8,128)(2,1)S(1)}, u32[]{:S(2)}, u32[]{:S(2)}) collective-permute-start(bf16[128,256]{1,0:T(8,128)(2,1)S(1)} %get-tuple-element.7), channel_id=1, source_target_pairs={{8,0},{16,8},{24,16},{32,24},{40,32},{48,40},{56,48},{64,56},{72,6... | collective-permute-start | bytes 196616 | tf_op jit(solution)/shard_map/ppermute | solution.py:444
  4.2 4.5 %collective-permute-start = (bf16[128,256]{1,0:T(8,128)(2,1)S(1)}, bf16[128,256]{1,0:T(8,128)(2,1)S(1)}, u32[]{:S(2)}, u32[]{:S(2)}) collective-permute-start(bf16[128,256]{1,0:T(8,128)(2,1)S(1)} %get-tuple-element.8), channel_id=1, source_target_pairs={{0,8},{8,16},{16,24},{24,32},{32,40},{40,48},{48,56},{56,64},{64,7... | collective-permute-start | bytes 196616 | tf_op jit(solution)/shard_map/ppermute | solution.py:443
  8.6 6.4 %copy-start.3 = (bf16[128,256]{1,0:T(8,128)(2,1)}, bf16[128,256]{1,0:T(8,128)(2,1)S(1)}, u32[]{:S(2)}) copy-start(bf16[128,256]{1,0:T(8,128)(2,1)S(1)} %collective-permute-done.1.below_ref) | copy-start | bytes 196612
  8.7 6.3 %copy-start.4 = (bf16[128,256]{1,0:T(8,128)(2,1)}, bf16[128,256]{1,0:T(8,128)(2,1)S(1)}, u32[]{:S(2)}) copy-start(bf16[128,256]{1,0:T(8,128)(2,1)S(1)} %collective-permute-done.above_ref) | copy-start | bytes 196612
  8.8 6.0 %collective-permute-start.3 = (bf16[40,256]{1,0:T(8,128)(2,1)S(1)}, bf16[40,256]{1,0:T(8,128)(2,1)S(1)}, u32[]{:S(2)}, u32[]{:S(2)}) collective-permute-start(bf16[40,256]{1,0:T(8,128)(2,1)S(1)} %get-tuple-element.13), channel_id=1, source_target_pairs={{1,0},{2,1},{3,2},{4,3},{5,4},{6,5},{7,6},{9,8},{10,9},{11,10},{12... | collective-permute-start | bytes 61448 | tf_op jit(solution)/shard_map/ppermute | solution.py:449
  10.1 4.9 %collective-permute-start.2 = (bf16[40,256]{1,0:T(8,128)(2,1)S(1)}, bf16[40,256]{1,0:T(8,128)(2,1)S(1)}, u32[]{:S(2)}, u32[]{:S(2)}) collective-permute-start(bf16[40,256]{1,0:T(8,128)(2,1)S(1)} %get-tuple-element.14), channel_id=1, source_target_pairs={{0,1},{1,2},{2,3},{3,4},{4,5},{5,6},{6,7},{8,9},{9,10},{10,11},{11... | collective-permute-start | bytes 61448 | tf_op jit(solution)/shard_map/ppermute | solution.py:448
  14.8 0.6 copy-start.5
  15.0 0.6 copy-start.6
  52.1 47.0 %copy-start = (bf16[2,256,768]{2,1,0:T(8,128)(2,1)S(1)}, bf16[2,256,768]{2,1,0:T(8,128)(2,1)}, u32[]{:S(2)}) copy-start(bf16[2,256,768]{2,1,0:T(8,128)(2,1)} %qkv_ref.3) | copy-start | bytes 2359300
  52.1 47.0 %copy-start.1 = (bf16[2,256,256]{2,1,0:T(8,128)(2,1)S(1)}, bf16[2,256,256]{2,1,0:T(8,128)(2,1)}, u32[]{:S(2)}) copy-start(bf16[2,256,256]{2,1,0:T(8,128)(2,1)} %wo_ref.3) | copy-start | bytes 786436
  52.1 47.0 %copy-start.2 = (f32[2,256]{1,0:T(2,128)S(1)}, f32[2,256]{1,0:T(2,128)}, u32[]{:S(2)}) copy-start(f32[2,256]{1,0:T(2,128)} %gain_ref.3) | copy-start | bytes 6148

commit v5 on v4

--- a/solution.py
+++ b/solution.py
@@ -440,13 +440,13 @@
 def halos(image):
     rows = lax.axis_size("row")
     cols = lax.axis_size("col")
-    above = lax.ppermute(image[-1], "row", [(i, i + 1) for i in range(rows - 1)])
-    below = lax.ppermute(image[0], "row", [(i + 1, i) for i in range(rows - 1)])
+    above = lax.ppermute(image[-1], "row", [(i, (i + 1) % rows) for i in range(rows)])
+    below = lax.ppermute(image[0], "row", [((i + 1) % rows, i) for i in range(rows)])
     none = jnp.zeros((38 - image.shape[0], image.shape[2]), image.dtype)
     first = jnp.concatenate([above[:1], image[:, 0], below[:1], none], axis=0)
     last = jnp.concatenate([above[-1:], image[:, -1], below[-1:], none], axis=0)
-    left = lax.ppermute(last, "col", [(i, i + 1) for i in range(cols - 1)])
-    right = lax.ppermute(first, "col", [(i + 1, i) for i in range(cols - 1)])
+    left = lax.ppermute(last, "col", [(i, (i + 1) % cols) for i in range(cols)])
+    right = lax.ppermute(first, "col", [((i + 1) % cols, i) for i in range(cols)])
     return above, below, left, right
 
 

time: 153 us -> 149 us (0.974)
  waiting for transfers between devices: 0.37 us -> 7.71 us
  blocking collectives: 81.5 us -> 74.2 us
  starting transfers between devices: 11.8 us -> 8.35 us
    ppermute x4, waiting for transfers between devices: 0.37 us -> 7.71 us  [the longest x1 5.34 us: halos(): left = lax.ppermute(last, 'col', [(i, (i + 1) % cols) for i in range(cols)])]
    all_to_all x1, blocking collectives: 47 us -> 39.7 us  [per_device(): lax.all_to_all(outgoing, ('row', 'col'), split_axis=0, concat_axis=0, til...]
    ppermute x4, starting transfers between devices: 11.8 us -> 8.35 us  [the longest x1 5.51 us: halos(): lax.ppermute(first, 'col', [((i + 1) % cols, i) for i in range(cols)])]
  transfers between devices with their start and end apart: 4 -> 4, of which waited for: 2 -> 4; matrix products, arithmetic and copies ran while one was open for 1% -> 1% of each run, Pallas kernels for 0% -> 0%
where the time goes in v5:
time: 149 us
  blocking collectives  74.2 us (50%)
  Pallas kernels  53.8 us (36%)
  starting transfers between devices  8.35 us (6%)
  waiting for transfers between devices  7.71 us (5%)
  local copies, waits for them, and re-layouts  4.22 us (3%)
    all_to_all x1, blocking collectives, per_device(): lax.all_to_all(outgoing, ('row', 'col'), split_axis=0, concat_axis=0, til...  39.7 us
    pallas_call x1, Pallas kernels, front(): pl.pallas_call(front_kernel, grid=(strips + 1,), in_specs=[pl.BlockSpec(m...  36.5 us
    all_to_all x1, blocking collectives, per_device(): lax.all_to_all(done.reshape(128, 32, chans), ('row', 'col'), split_axis=0...  34.6 us
    pallas_call x1, Pallas kernels, grid_attention(): pl.pallas_call(grid_kernel, grid=(1,), in_specs=[whole(tokens.shape), who...  17.3 us
    ppermute x1, starting transfers between devices, halos(): lax.ppermute(first, 'col', [((i + 1) % cols, i) for i in range(cols)])  5.51 us
    ppermute x1, waiting for transfers between devices, halos(): left = lax.ppermute(last, 'col', [(i, (i + 1) % cols) for i in range(cols)])  5.34 us
  transfers between devices with their start and end apart: 4, of which 4 were waited for; matrix products, arithmetic and copies ran while one was open for 1% of the time, Pallas kernels for 0%

profile of v5, /device:TPU:1, one launch (start us, length us, event | category | flops | bytes accessed | tf_op | source)
XLA Modules:
  0.0 149.1 jit_solution(6517841045832851196)
XLA Ops:
  0.0 0.9 slice_bitcast_fusion
  0.9 1.5 collective-permute-start.1
  2.4 1.3 collective-permute-start
  3.7 1.0 fusion
  4.8 0.1 pad.7.clone
  4.9 0.7 collective-permute-done.1.below_ref
  5.6 0.0 copy-start.3
  5.6 1.4 collective-permute-done.above_ref
  7.0 0.0 copy-start.4
  7.0 0.1 maximum_maximum_fusion.1
  7.1 5.5 %collective-permute-start.3 = (bf16[40,256]{1,0:T(8,128)(2,1)S(1)}, bf16[40,256]{1,0:T(8,128)(2,1)S(1)}, u32[]{:S(2)}, u32[]{:S(2)}) collective-permute-start(bf16[40,256]{1,0:T(8,128)(2,1)S(1)} %get-tuple-element.13), channel_id=1, source_target_pairs={{1,0},{2,1},{3,2},{4,3},{5,4},{6,5},{7,6},{0,7},{9,8},{10,9},{11,1... | collective-permute-start | bytes 61448 | tf_op jit(solution)/shard_map/ppermute | solution.py:449
  12.6 0.0 collective-permute-start.2
  12.6 0.7 add_convert_fusion.edge_ref
  13.3 0.2 collective-permute-done.3.right_ref
  13.5 0.0 copy-start.5
  13.5 5.3 %collective-permute-done.2.left_ref = bf16[40,256]{1,0:T(8,128)(2,1)S(1)} collective-permute-done((bf16[40,256]{1,0:T(8,128)(2,1)S(1)}, bf16[40,256]{1,0:T(8,128)(2,1)S(1)}, u32[]{:S(2)}, u32[]{:S(2)}) %collective-permute-start.2) | collective-permute-done | bytes 20512 | tf_op jit(solution)/shard_map/ppermute | solution.py:448
  18.9 0.0 copy-start.6
  18.9 0.0 copy-done.3
  18.9 0.0 copy-done.4
  18.9 0.0 copy-done.5
  18.9 0.6 copy-done.6
  19.5 36.5 %front.1 = bf16[4,8,4,2,16,256]{5,4,3,2,1,0:T(8,128)(2,1)} custom-call(s32[4]{0:T(128)} %add_convert_fusion.edge_ref, bf16[32,128,256]{2,1,0:T(8,128)(2,1)} %image_ref.1, bf16[128,256]{1,0:T(8,128)(2,1)} %copy-done.4, bf16[128,256]{1,0:T(8,128)(2,1)} %copy-done.3, bf16[40,256]{1,0:T(8,128)(2,1)} %copy-done.6, bf16[40,256]{1,0:T(8,128)(2,1)} %copy-done.5, ...), custom_call_target="tpu_custom_call" | custom-call | tf_op jit(solution)/shard_map/front/pallas_call | solution.py:396
  56.0 0.0 copy-start
  56.0 0.0 copy-start.1
  56.0 0.0 copy-start.2
  56.0 39.7 %all_to_all.10 = bf16[128,32,256]{2,1,0:T(8,128)(2,1)S(1)} all-to-all(bf16[128,32,256]{2,1,0:T(8,128)(2,1)} %bitcast.25), channel_id=1, replica_groups=mesh['row'=16,'col'=8] {'row','col'}, dimensions={0} | all-to-all | bytes 4194304 | tf_op jit(solution)/shard_map/all_to_all | solution.py:492
  95.6 0.0 copy-done
  95.6 0.0 copy-done.1
  95.6 0.0 copy-done.2
  95.7 17.3 %grid_attention.1 = bf16[256,16,256]{2,1,0:T(8,128)(2,1)S(1)} custom-call(bf16[256,16,256]{2,1,0:T(8,128)(2,1)S(1)} %bitcast.23, f32[2,256]{1,0:T(2,128)S(1)} %copy-done.2, bf16[2,256,768]{2,1,0:T(8,128)(2,1)S(1)} %copy-done, bf16[2,256,256]{2,1,0:T(8,128)(2,1)S(1)} %copy-done.1), custom_call_target="tpu_custom_call" | custom-call | tf_op jit(solution)/shard_map/grid_attention/pallas_call | solution.py:423
  112.9 34.6 %all_to_all.11 = bf16[128,32,256]{2,1,0:T(8,128)(2,1)S(1)} all-to-all(bf16[128,32,256]{2,1,0:T(8,128)(2,1)S(1)} %bitcast.24), channel_id=1, replica_groups=mesh['row'=16,'col'=8] {'row','col'}, dimensions={0} | all-to-all | bytes 4194304 | tf_op jit(solution)/shard_map/all_to_all | solution.py:494
  147.5 1.6 %copy.14 = bf16[4,8,4,2,2,8,256]{6,5,1,3,4,2,0:T(8,128)(2,1)} copy(bf16[4,8,4,2,2,8,256]{6,5,4,3,2,1,0:T(8,128)(2,1)S(1)} %bitcast.26) | data formatting | bytes 4194304 | tf_op jit(solution)/shard_map/reshape | solution.py:497
  (4 shorter events, 0.0 us)
Async XLA Ops:
  0.9 4.7 %collective-permute-start.1 = (bf16[128,256]{1,0:T(8,128)(2,1)S(1)}, bf16[128,256]{1,0:T(8,128)(2,1)S(1)}, u32[]{:S(2)}, u32[]{:S(2)}) collective-permute-start(bf16[128,256]{1,0:T(8,128)(2,1)S(1)} %get-tuple-element.7), channel_id=1, source_target_pairs={{8,0},{16,8},{24,16},{32,24},{40,32},{48,40},{56,48},{64,56},{72,6... | collective-permute-start | bytes 196616 | tf_op jit(solution)/shard_map/ppermute | solution.py:444
  2.4 4.6 %collective-permute-start = (bf16[128,256]{1,0:T(8,128)(2,1)S(1)}, bf16[128,256]{1,0:T(8,128)(2,1)S(1)}, u32[]{:S(2)}, u32[]{:S(2)}) collective-permute-start(bf16[128,256]{1,0:T(8,128)(2,1)S(1)} %get-tuple-element.8), channel_id=1, source_target_pairs={{0,8},{8,16},{16,24},{24,32},{32,40},{40,48},{48,56},{56,64},{64,7... | collective-permute-start | bytes 196616 | tf_op jit(solution)/shard_map/ppermute | solution.py:443
  5.6 13.3 %copy-start.3 = (bf16[128,256]{1,0:T(8,128)(2,1)}, bf16[128,256]{1,0:T(8,128)(2,1)S(1)}, u32[]{:S(2)}) copy-start(bf16[128,256]{1,0:T(8,128)(2,1)S(1)} %collective-permute-done.1.below_ref) | copy-start | bytes 196612
  7.0 11.9 %copy-start.4 = (bf16[128,256]{1,0:T(8,128)(2,1)}, bf16[128,256]{1,0:T(8,128)(2,1)S(1)}, u32[]{:S(2)}) copy-start(bf16[128,256]{1,0:T(8,128)(2,1)S(1)} %collective-permute-done.above_ref) | copy-start | bytes 196612
  7.1 6.4 %collective-permute-start.3 = (bf16[40,256]{1,0:T(8,128)(2,1)S(1)}, bf16[40,256]{1,0:T(8,128)(2,1)S(1)}, u32[]{:S(2)}, u32[]{:S(2)}) collective-permute-start(bf16[40,256]{1,0:T(8,128)(2,1)S(1)} %get-tuple-element.13), channel_id=1, source_target_pairs={{1,0},{2,1},{3,2},{4,3},{5,4},{6,5},{7,6},{0,7},{9,8},{10,9},{11,1... | collective-permute-start | bytes 61448 | tf_op jit(solution)/shard_map/ppermute | solution.py:449
  12.6 6.2 %collective-permute-start.2 = (bf16[40,256]{1,0:T(8,128)(2,1)S(1)}, bf16[40,256]{1,0:T(8,128)(2,1)S(1)}, u32[]{:S(2)}, u32[]{:S(2)}) collective-permute-start(bf16[40,256]{1,0:T(8,128)(2,1)S(1)} %get-tuple-element.14), channel_id=1, source_target_pairs={{0,1},{1,2},{2,3},{3,4},{4,5},{5,6},{6,7},{7,0},{8,9},{9,10},{10,1... | collective-permute-start | bytes 61448 | tf_op jit(solution)/shard_map/ppermute | solution.py:448
  13.5 5.3 %copy-start.5 = (bf16[40,256]{1,0:T(8,128)(2,1)}, bf16[40,256]{1,0:T(8,128)(2,1)S(1)}, u32[]{:S(2)}) copy-start(bf16[40,256]{1,0:T(8,128)(2,1)S(1)} %collective-permute-done.3.right_ref) | copy-start | bytes 61444
  18.9 0.6 copy-start.6
  56.0 39.7 %copy-start = (bf16[2,256,768]{2,1,0:T(8,128)(2,1)S(1)}, bf16[2,256,768]{2,1,0:T(8,128)(2,1)}, u32[]{:S(2)}) copy-start(bf16[2,256,768]{2,1,0:T(8,128)(2,1)} %qkv_ref.3) | copy-start | bytes 2359300
  56.0 39.7 %copy-start.1 = (bf16[2,256,256]{2,1,0:T(8,128)(2,1)S(1)}, bf16[2,256,256]{2,1,0:T(8,128)(2,1)}, u32[]{:S(2)}) copy-start(bf16[2,256,256]{2,1,0:T(8,128)(2,1)} %wo_ref.3) | copy-start | bytes 786436
  56.0 39.7 %copy-start.2 = (f32[2,256]{1,0:T(2,128)S(1)}, f32[2,256]{1,0:T(2,128)}, u32[]{:S(2)}) copy-start(f32[2,256]{1,0:T(2,128)} %gain_ref.3) | copy-start | bytes 6148

commit v6 on v5

--- a/solution.py
+++ b/solution.py
@@ -175,7 +175,6 @@
 
 
 def front_kernel(
-    edge_ref,
     image_ref,
     above_ref,
     below_ref,
@@ -201,6 +200,14 @@
     taps,
 ):
     step = pl.program_id(0)
+    row_at = lax.axis_index("row")
+    col_at = lax.axis_index("col")
+    edge_ref = [
+        jnp.where(row_at > 0, 1, 0),
+        jnp.where(row_at < lax.axis_size("row") - 1, 1, 0),
+        jnp.where(col_at > 0, 1, 0),
+        jnp.where(col_at < lax.axis_size("col") - 1, 1, 0),
+    ]
     rows_dev = image_ref.shape[0]
     strips = rows_dev // WINDOW
     cell = lax.broadcasted_iota(jnp.int32, (16, 1), 0)
@@ -389,15 +396,14 @@
     return pl.BlockSpec((1,) + shape[1:], lambda i: (n,) + (0,) * (len(shape) - 1))
 
 
-def front(edge, image, above, below, left, right, params):
+def front(image, above, below, left, right, params):
     rows_dev, cols_dev, chans = image.shape
     strips = rows_dev // WINDOW
     args = (image, above, below, left, right) + params
     return pl.pallas_call(
         front_kernel,
         grid=(strips + 1,),
-        in_specs=[pl.BlockSpec(memory_space=pltpu.SMEM)]
-        + [whole(a.shape) for a in args[:-2]]
+        in_specs=[whole(a.shape) for a in args[:-2]]
         + [layer(a.shape, 0) for a in args[-2:]],
         out_specs=pl.BlockSpec(
             (1, 8, 4, 2, 16, chans), lambda i: (jnp.maximum(i - 1, 0), 0, 0, 0, 0, 0)
@@ -416,7 +422,7 @@
             dimension_semantics=("arbitrary",), vmem_limit_bytes=60 * 2**20
         ),
         name="front",
-    )(edge, *args)
+    )(*args)
 
 
 def grid_attention(tokens, gain, qkv, wo):
@@ -464,16 +470,6 @@
     out_weight,
 ):
     rows_dev, cols_dev, chans = image.shape
-    row_at = lax.axis_index("row")
-    col_at = lax.axis_index("col")
-    edge = jnp.stack(
-        [
-            row_at > 0,
-            row_at < lax.axis_size("row") - 1,
-            col_at > 0,
-            col_at < lax.axis_size("col") - 1,
-        ]
-    ).astype(jnp.int32)
     above, below, left, right = halos(image)
     params = (
         bn_gain[None],
@@ -487,7 +483,7 @@
         qkv_weight,
         out_weight,
     )
-    after_block = front(edge, image, above, below, left, right, params)
+    after_block = front(image, above, below, left, right, params)
     outgoing = after_block.reshape(128, 32, chans)
     received = lax.all_to_all(outgoing, ("row", "col"), split_axis=0, concat_axis=0, tiled=True)
     done = grid_attention(received.reshape(256, 16, chans), norm_gain, qkv_weight, out_weight)

time: 149 us -> 149 us (level)
  no operation moved by 1% of the time
where the time goes in v6:
time: 149 us
  blocking collectives  74.3 us (50%)
  Pallas kernels  53.8 us (36%)
  waiting for transfers between devices  8.39 us (6%)
  starting transfers between devices  8.35 us (6%)
  local copies, waits for them, and re-layouts  4.22 us (3%)
    all_to_all x1, blocking collectives, per_device(): lax.all_to_all(outgoing, ('row', 'col'), split_axis=0, concat_axis=0, til...  39.7 us
    pallas_call x1, Pallas kernels, front(): pl.pallas_call(front_kernel, grid=(strips + 1,), in_specs=[whole(a.shape)...  36.5 us
    all_to_all x1, blocking collectives, per_device(): lax.all_to_all(done.reshape(128, 32, chans), ('row', 'col'), split_axis=0...  34.6 us
    pallas_call x1, Pallas kernels, grid_attention(): pl.pallas_call(grid_kernel, grid=(1,), in_specs=[whole(tokens.shape), who...  17.2 us
    ppermute x1, starting transfers between devices, halos(): lax.ppermute(first, 'col', [((i + 1) % cols, i) for i in range(cols)])  5.51 us
    ppermute x1, waiting for transfers between devices, halos(): left = lax.ppermute(last, 'col', [(i, (i + 1) % cols) for i in range(cols)])  5.34 us
  transfers between devices with their start and end apart: 4, of which 4 were waited for; matrix products, arithmetic and copies ran while one was open for 1% of the time, Pallas kernels for 0%

profile of v6, /device:TPU:1, one launch (start us, length us, event | category | flops | bytes accessed | tf_op | source)
XLA Modules:
  0.0 149.1 jit_solution(1350122637447427439)
XLA Ops:
  0.0 0.9 slice_bitcast_fusion
  0.9 1.5 collective-permute-start.1
  2.4 1.3 collective-permute-start
  3.7 1.0 fusion
  4.8 0.1 pad.7.clone
  4.9 0.7 collective-permute-done.1.below_ref
  5.6 0.0 copy-start.3
  5.6 1.4 collective-permute-done.above_ref
  7.0 0.0 copy-start.4
  7.0 0.1 maximum_maximum_fusion.1
  7.1 5.5 %collective-permute-start.3 = (bf16[40,256]{1,0:T(8,128)(2,1)S(1)}, bf16[40,256]{1,0:T(8,128)(2,1)S(1)}, u32[]{:S(2)}, u32[]{:S(2)}) collective-permute-start(bf16[40,256]{1,0:T(8,128)(2,1)S(1)} %get-tuple-element.13), channel_id=1, source_target_pairs={{1,0},{2,1},{3,2},{4,3},{5,4},{6,5},{7,6},{0,7},{9,8},{10,9},{11,1... | collective-permute-start | bytes 61448 | tf_op jit(solution)/shard_map/ppermute | solution.py:455
  12.6 0.0 collective-permute-start.2
  12.6 0.9 collective-permute-done.3.right_ref
  13.5 0.0 copy-start.5
  13.5 5.3 %collective-permute-done.2.left_ref = bf16[40,256]{1,0:T(8,128)(2,1)S(1)} collective-permute-done((bf16[40,256]{1,0:T(8,128)(2,1)S(1)}, bf16[40,256]{1,0:T(8,128)(2,1)S(1)}, u32[]{:S(2)}, u32[]{:S(2)}) %collective-permute-start.2) | collective-permute-done | bytes 20512 | tf_op jit(solution)/shard_map/ppermute | solution.py:454
  18.9 0.0 copy-start.6
  18.9 0.0 copy-done.3
  18.9 0.0 copy-done.4
  18.9 0.0 copy-done.5
  18.9 0.6 copy-done.6
  19.5 36.5 %front.1 = bf16[4,8,4,2,16,256]{5,4,3,2,1,0:T(8,128)(2,1)} custom-call(bf16[32,128,256]{2,1,0:T(8,128)(2,1)} %image_ref.1, bf16[128,256]{1,0:T(8,128)(2,1)} %copy-done.4, bf16[128,256]{1,0:T(8,128)(2,1)} %copy-done.3, bf16[40,256]{1,0:T(8,128)(2,1)} %copy-done.6, bf16[40,256]{1,0:T(8,128)(2,1)} %copy-done.5, f32[1,256]{1,0:T(1,128)} %bitcast.25, ...), custom_call_target="tpu_custom_call" | custom-call | tf_op jit(solution)/shard_map/front/pallas_call | solution.py:403
  56.0 0.0 copy-start
  56.0 0.0 copy-start.1
  56.0 0.0 copy-start.2
  56.0 39.7 %all_to_all.10 = bf16[128,32,256]{2,1,0:T(8,128)(2,1)S(1)} all-to-all(bf16[128,32,256]{2,1,0:T(8,128)(2,1)} %bitcast.21), channel_id=1, replica_groups=mesh['row'=16,'col'=8] {'row','col'}, dimensions={0} | all-to-all | bytes 4194304 | tf_op jit(solution)/shard_map/all_to_all | solution.py:488
  95.7 0.0 copy-done
  95.7 0.0 copy-done.1
  95.7 0.0 copy-done.2
  95.7 17.2 %grid_attention.1 = bf16[256,16,256]{2,1,0:T(8,128)(2,1)S(1)} custom-call(bf16[256,16,256]{2,1,0:T(8,128)(2,1)S(1)} %bitcast.19, f32[2,256]{1,0:T(2,128)S(1)} %copy-done.2, bf16[2,256,768]{2,1,0:T(8,128)(2,1)S(1)} %copy-done, bf16[2,256,256]{2,1,0:T(8,128)(2,1)S(1)} %copy-done.1), custom_call_target="tpu_custom_call" | custom-call | tf_op jit(solution)/shard_map/grid_attention/pallas_call | solution.py:429
  112.9 34.6 %all_to_all.11 = bf16[128,32,256]{2,1,0:T(8,128)(2,1)S(1)} all-to-all(bf16[128,32,256]{2,1,0:T(8,128)(2,1)S(1)} %bitcast.20), channel_id=1, replica_groups=mesh['row'=16,'col'=8] {'row','col'}, dimensions={0} | all-to-all | bytes 4194304 | tf_op jit(solution)/shard_map/all_to_all | solution.py:490
  147.5 1.6 %copy.14 = bf16[4,8,4,2,2,8,256]{6,5,1,3,4,2,0:T(8,128)(2,1)} copy(bf16[4,8,4,2,2,8,256]{6,5,4,3,2,1,0:T(8,128)(2,1)S(1)} %bitcast.22) | data formatting | bytes 4194304 | tf_op jit(solution)/shard_map/reshape | solution.py:493
  (4 shorter events, 0.0 us)
Async XLA Ops:
  0.9 4.7 %collective-permute-start.1 = (bf16[128,256]{1,0:T(8,128)(2,1)S(1)}, bf16[128,256]{1,0:T(8,128)(2,1)S(1)}, u32[]{:S(2)}, u32[]{:S(2)}) collective-permute-start(bf16[128,256]{1,0:T(8,128)(2,1)S(1)} %get-tuple-element.7), channel_id=1, source_target_pairs={{8,0},{16,8},{24,16},{32,24},{40,32},{48,40},{56,48},{64,56},{72,6... | collective-permute-start | bytes 196616 | tf_op jit(solution)/shard_map/ppermute | solution.py:450
  2.4 4.6 %collective-permute-start = (bf16[128,256]{1,0:T(8,128)(2,1)S(1)}, bf16[128,256]{1,0:T(8,128)(2,1)S(1)}, u32[]{:S(2)}, u32[]{:S(2)}) collective-permute-start(bf16[128,256]{1,0:T(8,128)(2,1)S(1)} %get-tuple-element.8), channel_id=1, source_target_pairs={{0,8},{8,16},{16,24},{24,32},{32,40},{40,48},{48,56},{56,64},{64,7... | collective-permute-start | bytes 196616 | tf_op jit(solution)/shard_map/ppermute | solution.py:449
  5.6 13.3 %copy-start.3 = (bf16[128,256]{1,0:T(8,128)(2,1)}, bf16[128,256]{1,0:T(8,128)(2,1)S(1)}, u32[]{:S(2)}) copy-start(bf16[128,256]{1,0:T(8,128)(2,1)S(1)} %collective-permute-done.1.below_ref) | copy-start | bytes 196612
  7.0 11.9 %copy-start.4 = (bf16[128,256]{1,0:T(8,128)(2,1)}, bf16[128,256]{1,0:T(8,128)(2,1)S(1)}, u32[]{:S(2)}) copy-start(bf16[128,256]{1,0:T(8,128)(2,1)S(1)} %collective-permute-done.above_ref) | copy-start | bytes 196612
  7.1 6.4 %collective-permute-start.3 = (bf16[40,256]{1,0:T(8,128)(2,1)S(1)}, bf16[40,256]{1,0:T(8,128)(2,1)S(1)}, u32[]{:S(2)}, u32[]{:S(2)}) collective-permute-start(bf16[40,256]{1,0:T(8,128)(2,1)S(1)} %get-tuple-element.13), channel_id=1, source_target_pairs={{1,0},{2,1},{3,2},{4,3},{5,4},{6,5},{7,6},{0,7},{9,8},{10,9},{11,1... | collective-permute-start | bytes 61448 | tf_op jit(solution)/shard_map/ppermute | solution.py:455
  12.6 6.2 %collective-permute-start.2 = (bf16[40,256]{1,0:T(8,128)(2,1)S(1)}, bf16[40,256]{1,0:T(8,128)(2,1)S(1)}, u32[]{:S(2)}, u32[]{:S(2)}) collective-permute-start(bf16[40,256]{1,0:T(8,128)(2,1)S(1)} %get-tuple-element.14), channel_id=1, source_target_pairs={{0,1},{1,2},{2,3},{3,4},{4,5},{5,6},{6,7},{7,0},{8,9},{9,10},{10,1... | collective-permute-start | bytes 61448 | tf_op jit(solution)/shard_map/ppermute | solution.py:454
  13.5 5.3 %copy-start.5 = (bf16[40,256]{1,0:T(8,128)(2,1)}, bf16[40,256]{1,0:T(8,128)(2,1)S(1)}, u32[]{:S(2)}) copy-start(bf16[40,256]{1,0:T(8,128)(2,1)S(1)} %collective-permute-done.3.right_ref) | copy-start | bytes 61444
  18.9 0.6 copy-start.6
  56.0 39.7 %copy-start = (bf16[2,256,768]{2,1,0:T(8,128)(2,1)S(1)}, bf16[2,256,768]{2,1,0:T(8,128)(2,1)}, u32[]{:S(2)}) copy-start(bf16[2,256,768]{2,1,0:T(8,128)(2,1)} %qkv_ref.3) | copy-start | bytes 2359300
  56.0 39.7 %copy-start.1 = (bf16[2,256,256]{2,1,0:T(8,128)(2,1)S(1)}, bf16[2,256,256]{2,1,0:T(8,128)(2,1)}, u32[]{:S(2)}) copy-start(bf16[2,256,256]{2,1,0:T(8,128)(2,1)} %wo_ref.3) | copy-start | bytes 786436
  56.0 39.7 %copy-start.2 = (f32[2,256]{1,0:T(2,128)S(1)}, f32[2,256]{1,0:T(2,128)}, u32[]{:S(2)}) copy-start(f32[2,256]{1,0:T(2,128)} %gain_ref.3) | copy-start | bytes 6148
